TPU v7x, 32 devices: a whole 2x2x4 slice. The times are simulated.
32 devices in a mesh: dp: 16 (over z, y, core), mp: 2 (over x).
Axes of the slice: x: 2, y: 2, z: 4, core: 2. Of those that a mesh axis runs over, the one named last changes fastest.
Arguments:
- tokens: bfloat16 [65536, 512], P(('dp', 'mp')), may hold values from -6 to 6
- out_grad: bfloat16 [65536, 512], P(('dp', 'mp')), may hold values from -6 to 6
- patch_valid: int32 [64, 256], P('dp'), may hold values 0 or 1
- clip_ids: int32 [64, 4], P('dp'), may hold values from 0 to 3, as said below
- ln_gain: float32 [2, 2, 512], replicated, may hold values from 0.1 to 1.9
- ln_bias: float32 [2, 2, 512], replicated, may hold values from -2 to 2
- w_qkv: bfloat16 [2, 512, 1536], P(None, None, 'mp'), may hold values from -0.25 to 0.25
- w_out: bfloat16 [2, 512, 512], P(None, 'mp'), may hold values from -0.5 to 0.5
- w_up: bfloat16 [2, 512, 2048], P(None, None, 'mp'), may hold values from -0.25 to 0.25
- w_down: bfloat16 [2, 2048, 512], P(None, 'mp'), may hold values from -0.125 to 0.125
Outputs:
- layer_out: bfloat16 [65536, 512], P(('dp', 'mp'))
- input_grad: float32 [65536, 512], P(('dp', 'mp'))
- grad_ln_gain: float32 [2, 2, 512], replicated
- grad_ln_bias: float32 [2, 2, 512], replicated
- grad_w_qkv: float32 [2, 512, 1536], P(None, None, 'mp')
- grad_w_out: float32 [2, 512, 512], P(None, 'mp')
- grad_w_up: float32 [2, 512, 2048], P(None, None, 'mp')
- grad_w_down: float32 [2, 2048, 512], P(None, 'mp')
Inputs may be any that keep to these rules, and one draw needn't show every extreme that they name: `clip_ids`: each stream's clip numbers start at 0 and rise by 0 or 1 from one frame slot to the next.
All inputs are finite; a program needn't handle non-finite values. No bound on the sum of `patch_valid` on one device may be relied on, other than what follows from the above.
Results may differ from a plain program's by a relative error of at most 0.025.
Values may be sent and summed in bfloat16 or wider, within the bound.
No kernel may reach another device: no remote copies, remote signals or barrier semaphores. Data moves between devices by JAX's collectives and lax.ppermute only.
A program may use at most 384 MiB of HBM per device.

v0:
```python
import jax
import jax.numpy as jnp
from jax import lax
from jax.sharding import PartitionSpec as P

HEAD_DIM = 64
FRAMES = 4


SPATIAL_FORMS = ("sfphe,sfqhe->sfhpq", "sfhpq,sfqhe->sfphe", "sfhpq,sfphe->sfqhe")
TEMPORAL_FORMS = ("sfphe,sgphe->sphfg", "sphfg,sgphe->sfphe", "sphfg,sfphe->sgphe")
ROWS_ONLY = (((0,), (0,)), ((), ()))
COLS_ONLY = (((1,), (1,)), ((), ()))


def layer_norm(values, ln_gain, ln_bias):
    centre = values - jnp.mean(values, axis=-1, keepdims=True)
    spread = jnp.mean(centre * centre, axis=-1, keepdims=True)
    return centre * lax.rsqrt(spread + 1e-05) * ln_gain + ln_bias


def mask_biases(patch_valid, clip_ids):
    space_bias = jnp.where(patch_valid == 1, 0.0, -1000000000.0).astype(jnp.float32)[
        :, None, None, None, :
    ]
    frame_row = jnp.arange(FRAMES)[:, None]
    frame_col = jnp.arange(FRAMES)[None, :]
    allowed = (clip_ids[:, :, None] == clip_ids[:, None, :]) & (frame_col <= frame_row)
    time_bias = jnp.where(allowed, 0.0, -1000000000.0).astype(jnp.float32)[:, None, None, :, :]
    return (space_bias, time_bias)


def norm_gather(normed):
    return lax.all_gather(normed, "mp", axis=0, tiled=True)


def grad_gather(grad_rows):
    return lax.all_gather(grad_rows, "mp", axis=0, tiled=True)


def branch_scatter(values_bf, weight):
    return lax.psum_scatter(
        jnp.dot(values_bf, weight, preferred_element_type=jnp.float32).astype(jnp.bfloat16),
        "mp",
        scatter_dimension=0,
        tiled=True,
    ).astype(jnp.float32)


def input_scatter(grads_bf, weight):
    return lax.psum_scatter(
        lax.dot_general(grads_bf, weight, COLS_ONLY, preferred_element_type=jnp.float32).astype(
            jnp.bfloat16
        ),
        "mp",
        scatter_dimension=0,
        tiled=True,
    ).astype(jnp.float32)


def weight_grad(stored, grads_bf):
    return lax.dot_general(stored, grads_bf, ROWS_ONLY, preferred_element_type=jnp.float32)


def split_heads(projected, streams, frames):
    heads_dev = projected.shape[1] // (3 * HEAD_DIM)
    split = projected.reshape(streams, frames, -1, heads_dev, 3, HEAD_DIM)
    return (split[..., 0, :], split[..., 1, :], split[..., 2, :], heads_dev)


def attend_forward(projected, mask_bias, einsum_forms, streams, frames):
    queries, key_rows, value_rows, heads_dev = split_heads(projected, streams, frames)
    scores = (
        jnp.einsum(einsum_forms[0], queries, key_rows, preferred_element_type=jnp.float32)
        * HEAD_DIM ** (-0.5)
        + mask_bias
    )
    top_score = jnp.max(scores, axis=-1, keepdims=True)
    exponent = jnp.exp(scores - top_score)
    total = jnp.sum(exponent, axis=-1, keepdims=True)
    weights = exponent / total
    log_total = top_score + jnp.log(total)
    mixed_heads = jnp.einsum(
        einsum_forms[1],
        weights.astype(jnp.bfloat16),
        value_rows,
        preferred_element_type=jnp.float32,
    )
    return (mixed_heads.astype(jnp.bfloat16).reshape(-1, heads_dev * HEAD_DIM), log_total)


def attend_backward(projected, log_total, heads_grad, mask_bias, einsum_forms, streams, frames):
    queries, key_rows, value_rows, heads_dev = split_heads(projected, streams, frames)
    grad_heads = heads_grad.reshape(streams, frames, -1, heads_dev, HEAD_DIM)
    scale = HEAD_DIM ** (-0.5)
    scores = (
        jnp.einsum(einsum_forms[0], queries, key_rows, preferred_element_type=jnp.float32) * scale
        + mask_bias
    )
    weights = jnp.exp(scores - log_total)
    weights_grad = jnp.einsum(
        einsum_forms[0], grad_heads, value_rows, preferred_element_type=jnp.float32
    )
    inner = jnp.sum(weights * weights_grad, axis=-1, keepdims=True)
    score_grad = (weights * (weights_grad - inner)).astype(jnp.bfloat16)
    query_grad = (
        jnp.einsum(einsum_forms[1], score_grad, key_rows, preferred_element_type=jnp.float32)
        * scale
    ).astype(jnp.bfloat16)
    key_grad = (
        jnp.einsum(einsum_forms[2], score_grad, queries, preferred_element_type=jnp.float32) * scale
    ).astype(jnp.bfloat16)
    value_grad = jnp.einsum(
        einsum_forms[2],
        weights.astype(jnp.bfloat16),
        grad_heads,
        preferred_element_type=jnp.float32,
    ).astype(jnp.bfloat16)
    return jnp.stack([query_grad, key_grad, value_grad], axis=-2).reshape(projected.shape)


def block_forward(
    stream_in,
    ln_gain,
    ln_bias,
    w_qkv,
    w_out,
    w_up,
    w_down,
    mask_bias,
    einsum_forms,
    streams,
    frames,
):
    normed = layer_norm(stream_in, ln_gain[0], ln_bias[0]).astype(jnp.bfloat16)
    full_rows = norm_gather(normed)
    projected = jnp.dot(full_rows, w_qkv, preferred_element_type=jnp.float32).astype(jnp.bfloat16)
    mixed_heads, log_total = attend_forward(projected, mask_bias, einsum_forms, streams, frames)
    middle = stream_in + branch_scatter(mixed_heads, w_out)
    second = layer_norm(middle, ln_gain[1], ln_bias[1]).astype(jnp.bfloat16)
    second_full = norm_gather(second)
    hidden_pre = jnp.dot(second_full, w_up, preferred_element_type=jnp.float32)
    activated = jax.nn.gelu(hidden_pre).astype(jnp.bfloat16)
    result = middle + branch_scatter(activated, w_down)
    kept = (
        stream_in,
        full_rows,
        projected,
        mixed_heads,
        log_total,
        middle,
        second_full,
        hidden_pre,
        activated,
    )
    return (result, kept)


def block_backward(
    result_grad,
    kept,
    ln_gain,
    ln_bias,
    w_qkv,
    w_out,
    w_up,
    w_down,
    mask_bias,
    einsum_forms,
    streams,
    frames,
):
    (
        stream_in,
        first_store,
        projected,
        mixed_heads,
        log_total,
        middle,
        second_store,
        hidden_pre,
        activated,
    ) = kept
    result_low = result_grad.astype(jnp.bfloat16)
    gelu_pull = jax.vjp(jax.nn.gelu, hidden_pre)[1]
    down_in = grad_gather(result_low)
    grad_down = lax.dot_general(activated, down_in, ROWS_ONLY, preferred_element_type=jnp.float32)
    act_grad = lax.dot_general(down_in, w_down, COLS_ONLY, preferred_element_type=jnp.float32)
    hidden_grad = gelu_pull(act_grad)[0].astype(jnp.bfloat16)
    grad_up = weight_grad(second_store, hidden_grad)
    second_grad = input_scatter(hidden_grad, w_up)
    second_pull = jax.vjp(layer_norm, middle, ln_gain[1], ln_bias[1])[1]
    middle_part, gain_two, shift_two = second_pull(second_grad)
    middle_grad = result_grad + middle_part
    middle_low = middle_grad.astype(jnp.bfloat16)
    out_in = grad_gather(middle_low)
    grad_out = lax.dot_general(mixed_heads, out_in, ROWS_ONLY, preferred_element_type=jnp.float32)
    heads_grad = lax.dot_general(
        out_in, w_out, COLS_ONLY, preferred_element_type=jnp.float32
    ).astype(jnp.bfloat16)
    proj_grad = attend_backward(
        projected, log_total, heads_grad, mask_bias, einsum_forms, streams, frames
    )
    grad_qkv = weight_grad(first_store, proj_grad)
    first_grad = input_scatter(proj_grad, w_qkv)
    first_pull = jax.vjp(layer_norm, stream_in, ln_gain[0], ln_bias[0])[1]
    input_part, gain_one, shift_one = first_pull(first_grad)
    matrices = (grad_qkv, grad_out, grad_up, grad_down)
    return (
        middle_grad + input_part,
        matrices,
        jnp.stack([gain_one, gain_two]),
        jnp.stack([shift_one, shift_two]),
    )


def shards(tokens, out_grad, patch_valid, clip_ids, ln_gain, ln_bias, w_qkv, w_out, w_up, w_down):
    streams = patch_valid.shape[0]
    space_bias, time_bias = mask_biases(patch_valid, clip_ids)
    up_use, down_use = (w_up, w_down)
    weights = (w_qkv, w_out, up_use, down_use)
    layouts = ((streams, FRAMES, space_bias), (streams, FRAMES, time_bias))
    form_pair = (SPATIAL_FORMS, TEMPORAL_FORMS)
    state = tokens.astype(jnp.float32)
    kept_blocks = []
    for layer_index in range(2):
        group_count, frame_count, mask_bias = layouts[layer_index]
        state, kept = block_forward(
            state,
            ln_gain[layer_index],
            ln_bias[layer_index],
            weights[0][layer_index],
            weights[1][layer_index],
            weights[2][layer_index],
            weights[3][layer_index],
            mask_bias,
            form_pair[layer_index],
            group_count,
            frame_count,
        )
        kept_blocks.append(kept)
    layer_out = state.astype(jnp.bfloat16)
    grad_state = out_grad.astype(jnp.float32)
    matrix_grads = [None, None]
    gain_grads = [None, None]
    shift_grads = [None, None]
    for layer_index in (1, 0):
        group_count, frame_count, mask_bias = layouts[layer_index]
        grad_state, matrices, gain_part, shift_part = block_backward(
            grad_state,
            kept_blocks[layer_index],
            ln_gain[layer_index],
            ln_bias[layer_index],
            weights[0][layer_index],
            weights[1][layer_index],
            weights[2][layer_index],
            weights[3][layer_index],
            mask_bias,
            form_pair[layer_index],
            group_count,
            frame_count,
        )
        matrix_grads[layer_index] = matrices
        gain_grads[layer_index] = gain_part
        shift_grads[layer_index] = shift_part
    stacked = tuple(
        (jnp.stack([matrix_grads[0][item], matrix_grads[1][item]]) for item in range(4))
    )
    stacked = (
        lax.psum(stacked[0].astype(jnp.bfloat16), "dp").astype(jnp.float32),
        lax.psum(stacked[1].astype(jnp.bfloat16), "dp").astype(jnp.float32),
        lax.psum(stacked[2].astype(jnp.bfloat16), "dp").astype(jnp.float32),
        lax.psum(stacked[3].astype(jnp.bfloat16), "dp").astype(jnp.float32),
    )
    norm_sums = lax.psum((jnp.stack(gain_grads), jnp.stack(shift_grads)), ("dp", "mp"))
    return (
        layer_out,
        grad_state,
        norm_sums[0],
        norm_sums[1],
        stacked[0],
        stacked[1],
        stacked[2],
        stacked[3],
    )


def solution(mesh):
    return jax.shard_map(
        shards,
        mesh=mesh,
        in_specs=(
            P(("dp", "mp"), None),
            P(("dp", "mp"), None),
            P("dp", None),
            P("dp", None),
            P(),
            P(),
            P(None, None, "mp"),
            P(None, "mp", None),
            P(None, None, "mp"),
            P(None, "mp", None),
        ),
        out_specs=(
            P(("dp", "mp"), None),
            P(("dp", "mp"), None),
            P(),
            P(),
            P(None, None, "mp"),
            P(None, "mp", None),
            P(None, None, "mp"),
            P(None, "mp", None),
        ),
        check_vma=False,
    )
```

profile of v0, /device:TPU:0, one launch (start us, length us, event | category | flops | bytes accessed | tf_op | source)
XLA Modules:
  0.0 1633.3 jit_solution(12038300688431298814)
XLA Ops:
  15.6 59.5 %all-gather.9.cloned.1.call-done = bf16[4096,512]{1,0:T(8,128)(2,1)} async-done(((bf16[2048,512]{1,0:T(8,128)(2,1)}), bf16[4096,512]{1,0:T(8,128)(2,1)}) %all-gather.9.cloned.1.call-update) | async-done | bytes 4194320 | tf_op jit(solution)/shard_map/all_gather | solution.py:34
  92.2 11.2 reshape.234
  149.7 54.0 %reduce-scatter.9.cloned.1.call-done = bf16[2048,512]{1,0:T(8,128)(2,1)} async-done(((bf16[4096,512]{1,0:T(8,128)(2,1)}), bf16[2048,512]{1,0:T(8,128)(2,1)}) %reduce-scatter.9.cloned.1.call-update) | async-done | bytes 2097168 | tf_op jit(solution)/shard_map/reduce_scatter | solution.py:42
  210.5 56.9 %all-gather.11.cloned.1.call-done = bf16[4096,512]{1,0:T(8,128)(2,1)} async-done(((bf16[2048,512]{1,0:T(8,128)(2,1)}), bf16[4096,512]{1,0:T(8,128)(2,1)}) %all-gather.11.cloned.1.call-update) | async-done | bytes 4194320 | tf_op jit(solution)/shard_map/all_gather | solution.py:34
  267.3 12.9 multiply_convert_fusion.2
  289.6 54.4 %reduce-scatter.11.cloned.1.call-done = bf16[2048,512]{1,0:T(8,128)(2,1)} async-done(((bf16[4096,512]{1,0:T(8,128)(2,1)}), bf16[2048,512]{1,0:T(8,128)(2,1)}) %reduce-scatter.11.cloned.1.call-update) | async-done | bytes 2097168 | tf_op jit(solution)/shard_map/reduce_scatter | solution.py:42
  351.6 56.8 %all-gather.13.cloned.1.call-done = bf16[4096,512]{1,0:T(8,128)(2,1)} async-done(((bf16[2048,512]{1,0:T(8,128)(2,1)}), bf16[4096,512]{1,0:T(8,128)(2,1)}) %all-gather.13.cloned.1.call-update) | async-done | bytes 4194320 | tf_op jit(solution)/shard_map/all_gather | solution.py:34
  425.3 11.1 reshape.236
  463.9 12.3 fusion.137
  511.3 53.6 %reduce-scatter.13.cloned.1.call-done = bf16[2048,512]{1,0:T(8,128)(2,1)} async-done(((bf16[4096,512]{1,0:T(8,128)(2,1)}), bf16[2048,512]{1,0:T(8,128)(2,1)}) %reduce-scatter.13.cloned.1.call-update) | async-done | bytes 2097168 | tf_op jit(solution)/shard_map/reduce_scatter | solution.py:42
  572.1 51.2 %all-gather.17.cloned.1.call-done = bf16[4096,512]{1,0:T(8,128)(2,1)} async-done(((bf16[2048,512]{1,0:T(8,128)(2,1)}), bf16[4096,512]{1,0:T(8,128)(2,1)}) %all-gather.17.cloned.1.call-update) | async-done | bytes 4194320 | tf_op jit(solution)/shard_map/all_gather | solution.py:38
  623.3 14.6 fusion.85
  637.9 44.3 %all-gather.15.cloned.1.call-done = bf16[4096,512]{1,0:T(8,128)(2,1)} async-done(((bf16[2048,512]{1,0:T(8,128)(2,1)}), bf16[4096,512]{1,0:T(8,128)(2,1)}) %all-gather.15.cloned.1.call-update) | async-done | bytes 4194320 | tf_op jit(solution)/shard_map/all_gather | solution.py:34
  682.3 20.2 %fusion.13 = (bf16[4096,1024]{1,0:T(8,128)(2,1)S(1)}, bf16[4096,1024]{1,0:T(8,128)(2,1)}) fusion(f32[4096,1024]{1,0:T(8,128)} %fusion.85, bf16[4096,512]{1,0:T(8,128)(2,1)} %all-gather.15.cloned.1.call-done, bf16[2,512,1024]{2,1,0:T(8,128)(2,1)} %param.18), kind=kOutput, calls=%fused_computation.17 | convolution fusion | flops 4387241984 | bytes 38797312 | tf_op jit(solution)/shard_map/dot_general | solution.py:142
  722.8 44.1 %reduce-scatter.17.cloned.1.call-done = bf16[2048,512]{1,0:T(8,128)(2,1)} async-done(((bf16[4096,512]{1,0:T(8,128)(2,1)}), bf16[2048,512]{1,0:T(8,128)(2,1)}) %reduce-scatter.17.cloned.1.call-update) | async-done | bytes 2097168 | tf_op jit(solution)/shard_map/reduce_scatter | solution.py:51
  771.5 51.9 %reduce-scatter.15.cloned.1.call-done = bf16[2048,512]{1,0:T(8,128)(2,1)} async-done(((bf16[4096,512]{1,0:T(8,128)(2,1)}), bf16[2048,512]{1,0:T(8,128)(2,1)}) %reduce-scatter.15.cloned.1.call-update) | async-done | bytes 2097168 | tf_op jit(solution)/shard_map/reduce_scatter | solution.py:42
  836.5 53.0 %all-gather.19.cloned.1.call-done = bf16[4096,512]{1,0:T(8,128)(2,1)} async-done(((bf16[2048,512]{1,0:T(8,128)(2,1)}), bf16[4096,512]{1,0:T(8,128)(2,1)}) %all-gather.19.cloned.1.call-update) | async-done | bytes 4194320 | tf_op jit(solution)/shard_map/all_gather | solution.py:38
  912.5 16.7 %multiply_reduce_fusion.1 = (f32[4,256,4,4]{3,2,1,0:T(4,128)}, f32[4,256,4,4,4]{3,4,2,1,0:T(4,128)}) fusion(f32[4,256,4,4,4]{3,4,2,1,0:T(4,128)} %get-tuple-element.59, f32[4,256,4,4]{3,2,1,0:T(4,128)} %bitcast.220, bf16[4,4,256,4,1,64]{5,1,3,2,0,4:T(4,128)(2,1)} %copy.71, bf16[4,4,256,4,64]{4,3,2,1,0:T(4,128)(2,1)} %reshape.250), kind=kOutput, calls=%fused_computation.34 | convolution fusion | flops 8568832 | bytes 4849664 | tf_op jit(solution)/shard_map/sfphe,sgphe->sphfg/dot_general | solution.py:101
  953.7 13.3 pad_maximum_fusion
  967.1 20.2 %copy.50 = bf16[4,4,256,4,3,64]{2,1,0,5,4,3:T(4,128)(2,1)} copy(bf16[4,4,256,4,3,64]{5,1,3,2,0,4:T(4,128)(2,1)} %pad_maximum_fusion) | data formatting | bytes 12582912 | tf_op jit(solution)/shard_map/stack | solution.py:119
  987.3 11.1 reshape.239
  1007.0 54.4 %reduce-scatter.19.cloned.1.call-done = bf16[2048,512]{1,0:T(8,128)(2,1)} async-done(((bf16[4096,512]{1,0:T(8,128)(2,1)}), bf16[2048,512]{1,0:T(8,128)(2,1)}) %reduce-scatter.19.cloned.1.call-update) | async-done | bytes 2097168 | tf_op jit(solution)/shard_map/reduce_scatter | solution.py:51
  1073.6 56.9 %all-gather.21.cloned.1.call-done = bf16[4096,512]{1,0:T(8,128)(2,1)} async-done(((bf16[2048,512]{1,0:T(8,128)(2,1)}), bf16[4096,512]{1,0:T(8,128)(2,1)}) %all-gather.21.cloned.1.call-update) | async-done | bytes 4194320 | tf_op jit(solution)/shard_map/all_gather | solution.py:38
  1130.5 17.1 %fusion.6 = bf16[4096,1024]{1,0:T(8,128)(2,1)S(1)} fusion(f32[4096,1024]{1,0:T(8,128)} %get-tuple-element.57, bf16[4096,512]{1,0:T(8,128)(2,1)} %all-gather.21.cloned.1.call-done, bf16[2,1024,512]{2,1,0:T(8,128)(2,1)} %param.19), kind=kOutput, calls=%fused_computation.10 | convolution fusion | flops 4378853376 | bytes 30408704 | tf_op jit(solution)/shard_map/dot_general | solution.py:188
  1175.9 35.5 %reduce-scatter.21.cloned.1.call-done = bf16[2048,512]{1,0:T(8,128)(2,1)} async-done(((bf16[4096,512]{1,0:T(8,128)(2,1)}), bf16[2048,512]{1,0:T(8,128)(2,1)}) %reduce-scatter.21.cloned.1.call-update) | async-done | bytes 2097168 | tf_op jit(solution)/shard_map/reduce_scatter | solution.py:51
  1246.0 32.0 %all-gather.23.cloned.1.call-done = bf16[4096,512]{1,0:T(8,128)(2,1)} async-done(((bf16[2048,512]{1,0:T(8,128)(2,1)}), bf16[4096,512]{1,0:T(8,128)(2,1)}) %all-gather.23.cloned.1.call-update) | async-done | bytes 4194320 | tf_op jit(solution)/shard_map/all_gather | solution.py:38
  1306.0 11.7 multiply_reduce_fusion
  1317.6 11.9 multiply_convert_fusion
  1351.9 11.2 reshape.241
  1383.9 131.7 %all-reduce.4.cloned.1.call-done = (bf16[2,512,768]{2,1,0:T(8,128)(2,1)}, bf16[2,256,512]{2,1,0:T(8,128)(2,1)}, bf16[2,512,1024]{2,1,0:T(8,128)(2,1)}, bf16[2,1024,512]{2,1,0:T(8,128)(2,1)}) async-done(((bf16[2,512,768]{2,1,0:T(8,128)(2,1)}, bf16[2,256,512]{2,1,0:T(8,128)(2,1)}, bf16[2,512,1024]{2,1,0:T(8,128)(2,1)}, bf16[2,1024,512]{2,1,0:T(8,128)(2,1)}), (bf16[2,512,768]{2,1,0:T(8,128)(2,1)}, ...) | async-done | bytes 6291472 | tf_op jit(solution)/shard_map/psum | solution.py:270
  1526.3 45.8 %reduce-scatter.23.cloned.1.call-done = bf16[2048,512]{1,0:T(8,128)(2,1)} async-done(((bf16[4096,512]{1,0:T(8,128)(2,1)}), bf16[2048,512]{1,0:T(8,128)(2,1)}) %reduce-scatter.23.cloned.1.call-update) | async-done | bytes 2097168 | tf_op jit(solution)/shard_map/reduce_scatter | solution.py:51
  1578.3 39.5 %all-reduce = (f32[2,2,512]{2,1,0:T(2,128)}, f32[2,2,512]{2,1,0:T(2,128)}) all-reduce(f32[2,2,512]{2,1,0:T(2,128)S(1)} %pad_maximum_fusion.6, f32[2,2,512]{2,1,0:T(2,128)S(1)} %pad_maximum_fusion.7), channel_id=1, replica_groups=mesh['dp'=16,'mp'=2] {'dp','mp'}, use_global_device_ids=true, to_apply=%region_34.35 | all-reduce | flops 4096 | bytes 32768 | tf_op jit(solution)/shard_map/psum | solution.py:275
  (325 shorter events, 446.8 us)
Async XLA Ops:
  7.2 68.0 %all-gather.9.cloned.1.call-start = ((), (), s32[]{:S(2)}) async-start(), calls=%async_computation.8 | async-start | bytes 6291456 | tf_op jit(solution)/shard_map/all_gather | solution.py:34
  13.0 194.7 %copy-start.60 = (f32[1,1,512]{2,1,0:T(1,128)}, f32[1,1,512]{2,1,0:T(1,128)S(1)}, u32[]{:S(2)}) copy-start(f32[1,1,512]{2,1,0:T(1,128)S(1)} %get-tuple-element.47) | copy-start | bytes 6148
  13.1 336.0 %copy-start.64 = (f32[1,1,512]{2,1,0:T(1,128)}, f32[1,1,512]{2,1,0:T(1,128)S(1)}, u32[]{:S(2)}) copy-start(f32[1,1,512]{2,1,0:T(1,128)S(1)} %get-tuple-element.49) | copy-start | bytes 6148
  15.6 188.1 %reduce-scatter.9.cloned.1.call-start = ((), (), s32[]{:S(2)}) async-start(), calls=%async_computation.9 | async-start | bytes 6291456 | tf_op jit(solution)/shard_map/reduce_scatter | solution.py:42
  149.2 118.1 %all-gather.11.cloned.1.call-start = ((), (), s32[]{:S(2)}) async-start(), calls=%async_computation.10 | async-start | bytes 6291456 | tf_op jit(solution)/shard_map/all_gather | solution.py:34
  210.4 133.6 %reduce-scatter.11.cloned.1.call-start = ((), (), s32[]{:S(2)}) async-start(), calls=%async_computation.11 | async-start | bytes 6291456 | tf_op jit(solution)/shard_map/reduce_scatter | solution.py:42
  289.5 118.9 %all-gather.13.cloned.1.call-start = ((), (), s32[]{:S(2)}) async-start(), calls=%async_computation.12 | async-start | bytes 6291456 | tf_op jit(solution)/shard_map/all_gather | solution.py:34
  349.7 58.7 %copy-start.83 = (bf16[2,512,768]{2,1,0:T(8,128)(2,1)S(1)}, bf16[2,512,768]{2,1,0:T(8,128)(2,1)}, u32[]{:S(2)}) copy-start(bf16[2,512,768]{2,1,0:T(8,128)(2,1)} %param.16) | copy-start | bytes 4718596
  351.5 213.5 %reduce-scatter.13.cloned.1.call-start = ((), (), s32[]{:S(2)}) async-start(), calls=%async_computation.13 | async-start | bytes 6291456 | tf_op jit(solution)/shard_map/reduce_scatter | solution.py:42
  510.5 112.8 %all-gather.17.cloned.1.call-start = ((), (), s32[]{:S(2)}) async-start(), calls=%async_computation.16 | async-start | bytes 6291456 | tf_op jit(solution)/shard_map/all_gather | solution.py:38
  511.2 171.1 %all-gather.15.cloned.1.call-start = ((), (), s32[]{:S(2)}) async-start(), calls=%async_computation.14 | async-start | bytes 6291456 | tf_op jit(solution)/shard_map/all_gather | solution.py:34
  572.0 194.8 %reduce-scatter.17.cloned.1.call-start = ((), (), s32[]{:S(2)}) async-start(), calls=%async_computation.17 | async-start | bytes 6291456 | tf_op jit(solution)/shard_map/reduce_scatter | solution.py:51
  712.4 110.9 %reduce-scatter.15.cloned.1.call-start = ((), (), s32[]{:S(2)}) async-start(), calls=%async_computation.15 | async-start | bytes 6291456 | tf_op jit(solution)/shard_map/reduce_scatter | solution.py:42
  722.7 166.8 %all-gather.19.cloned.1.call-start = ((), (), s32[]{:S(2)}) async-start(), calls=%async_computation.18 | async-start | bytes 6291456 | tf_op jit(solution)/shard_map/all_gather | solution.py:38
  771.4 59.2 %copy-start.15 = (bf16[2048,512]{1,0:T(8,128)(2,1)S(1)}, bf16[2048,512]{1,0:T(8,128)(2,1)}, u32[]{:S(2)}) copy-start(bf16[2048,512]{1,0:T(8,128)(2,1)} %param.11) | copy-start | bytes 6291460
  832.6 228.7 %reduce-scatter.19.cloned.1.call-start = ((), (), s32[]{:S(2)}) async-start(), calls=%async_computation.19 | async-start | bytes 6291456 | tf_op jit(solution)/shard_map/reduce_scatter | solution.py:51
  1006.9 54.5 %copy-start.45 = (f32[2048]{0:T(1024)S(1)}, f32[2048]{0:T(1024)}, u32[]{:S(2)}) copy-start(f32[2048]{0:T(1024)} %copy-done.44) | copy-start | bytes 24580
  1006.9 54.5 %copy-start.65 = (f32[1,1,512]{2,1,0:T(1,128)S(1)}, f32[1,1,512]{2,1,0:T(1,128)}, u32[]{:S(2)}) copy-start(f32[1,1,512]{2,1,0:T(1,128)} %copy-done.64) | copy-start | bytes 6148
  1006.9 59.8 %copy-start.59 = (f32[2048]{0:T(1024)S(1)}, f32[2048]{0:T(1024)}, u32[]{:S(2)}) copy-start(f32[2048]{0:T(1024)} %copy-done.58) | copy-start | bytes 24580
  1006.9 59.8 %copy-start.53 = (f32[2048]{0:T(1024)S(1)}, f32[2048]{0:T(1024)}, u32[]{:S(2)}) copy-start(f32[2048]{0:T(1024)} %copy-done.52) | copy-start | bytes 24580
  1006.9 123.5 %all-gather.21.cloned.1.call-start = ((), (), s32[]{:S(2)}) async-start(), calls=%async_computation.20 | async-start | bytes 6291456 | tf_op jit(solution)/shard_map/all_gather | solution.py:38
  1073.6 137.9 %reduce-scatter.21.cloned.1.call-start = ((), (), s32[]{:S(2)}) async-start(), calls=%async_computation.21 | async-start | bytes 6291456 | tf_op jit(solution)/shard_map/reduce_scatter | solution.py:51
  1157.0 120.9 %all-gather.23.cloned.1.call-start = ((), (), s32[]{:S(2)}) async-start(), calls=%async_computation.22 | async-start | bytes 6291456 | tf_op jit(solution)/shard_map/all_gather | solution.py:38
  1221.0 294.6 %all-reduce.4.cloned.1.call-start = ((), (), s32[]{:S(2)}) async-start(), calls=%async_computation.24 | async-start | bytes 12582912 | tf_op jit(solution)/shard_map/psum | solution.py:270
  1375.3 196.8 %reduce-scatter.23.cloned.1.call-start = ((), (), s32[]{:S(2)}) async-start(), calls=%async_computation.23 | async-start | bytes 6291456 | tf_op jit(solution)/shard_map/reduce_scatter | solution.py:51
  1523.7 48.4 %copy-start.63 = (f32[1,1,512]{2,1,0:T(1,128)S(1)}, f32[1,1,512]{2,1,0:T(1,128)}, u32[]{:S(2)}) copy-start(f32[1,1,512]{2,1,0:T(1,128)} %copy-done.62) | copy-start | bytes 6148
  1523.7 51.8 %copy-start.55 = (f32[2048]{0:T(1024)S(1)}, f32[2048]{0:T(1024)}, u32[]{:S(2)}) copy-start(f32[2048]{0:T(1024)} %copy-done.54) | copy-start | bytes 24580
  1523.7 51.8 %copy-start.51 = (f32[2048]{0:T(1024)S(1)}, f32[2048]{0:T(1024)}, u32[]{:S(2)}) copy-start(f32[2048]{0:T(1024)} %copy-done.50) | copy-start | bytes 24580
  1526.3 51.9 %copy-start.68 = (f32[512]{0:T(512)S(1)}, f32[512]{0:T(512)}, u32[]{:S(2)}) copy-start(f32[512]{0:T(512)} %get-tuple-element.22) | copy-start | bytes 6148
  1526.3 51.9 %copy-start.70 = (f32[512]{0:T(512)S(1)}, f32[512]{0:T(512)}, u32[]{:S(2)}) copy-start(f32[512]{0:T(512)} %get-tuple-element.20) | copy-start | bytes 6148
  1526.3 52.0 %copy-start.67 = (f32[512]{0:T(512)S(1)}, f32[512]{0:T(512)}, u32[]{:S(2)}) copy-start(f32[512]{0:T(512)} %get-tuple-element.12) | copy-start | bytes 6148
  1526.3 52.0 %copy-start.69 = (f32[512]{0:T(512)S(1)}, f32[512]{0:T(512)}, u32[]{:S(2)}) copy-start(f32[512]{0:T(512)} %get-tuple-element.10) | copy-start | bytes 6148
  (76 other events, 666.8 us)
Sparse Core Ops, SparseCore 0:
  15.7 59.4 all-gather.8
  149.3 54.2 reduce-scatter.8
  210.5 56.7 all-gather.10
  289.6 54.3 reduce-scatter.10
  351.6 56.7 all-gather.12
  510.6 54.2 reduce-scatter.12
  566.5 56.7 all-gather.16
  625.5 56.7 all-gather.14
  712.5 54.3 reduce-scatter.16
  769.0 54.2 reduce-scatter.14
  832.8 56.7 all-gather.18
  1007.0 54.3 reduce-scatter.18
  1073.7 56.7 all-gather.20
  1157.1 54.2 reduce-scatter.20
  1221.1 56.7 all-gather.22
  1375.4 140.1 all-reduce.3
  1517.7 54.3 reduce-scatter.22
where the time goes:
time: 1640 us; the launch traced here: 1630 us
  waiting for transfers between devices  937 us (57%)
  matrix products  302 us (18%)
  local copies, waits for them, and re-layouts  187 us (11%)
  other arithmetic  151 us (9%)
  blocking collectives  39.5 us (2%)
    all_gather x4, waiting for transfers between devices, norm_gather(): return lax.all_gather(normed, 'mp', axis=0, tiled=True)  217 us
    reduce_scatter x4, waiting for transfers between devices, branch_scatter(): lax.psum_scatter(jnp.dot(values_bf, weight, preferred_element_type=jnp.fl...  214 us
    all_gather x4, waiting for transfers between devices, grad_gather(): return lax.all_gather(grad_rows, 'mp', axis=0, tiled=True)  193 us
    reduce_scatter x4, waiting for transfers between devices, input_scatter(): lax.psum_scatter(lax.dot_general(grads_bf, weight, COLS_ONLY, preferred_e...  180 us
    psum x1, waiting for transfers between devices, shards(): lax.psum(stacked[0].astype(jnp.bfloat16), 'dp').astype(jnp.float32)  132 us
    unnamed x185, local copies, waits for them, and re-layouts  43.4 us
    psum x1, blocking collectives, shards(): lax.psum((jnp.stack(gain_grads), jnp.stack(shift_grads)), ('dp', 'mp'))  39.5 us
    dot_general x2, matrix products, block_forward(): hidden_pre = jnp.dot(second_full, w_up, preferred_element_type=jnp.float32)  33.1 us
  transfers between devices with their start and end apart: 17, of which 17 were waited for; matrix products, arithmetic and copies ran while one was open for 6% of the time, Pallas kernels for 0%

commit v1 on v0

--- a/solution.py
+++ b/solution.py
@@ -1,10 +1,715 @@
+import functools
+
 import jax
 import jax.numpy as jnp
 from jax import lax
+from jax.experimental import pallas as pl
+from jax.experimental.pallas import tpu as pltpu
+from jax.sharding import Mesh
 from jax.sharding import PartitionSpec as P
 
 HEAD_DIM = 64
 FRAMES = 4
+EPS = 1e-05
+SCALE = HEAD_DIM ** (-0.5)
+F32 = jnp.float32
+BF = jnp.bfloat16
+VMEM_BYTES = 56 * 2**20
+SWAP = [(0, 1), (1, 0)]
+
+
+def nn(a, b):
+    return lax.dot_general(a, b, (((1,), (0,)), ((), ())), preferred_element_type=F32)
+
+
+def nt(a, b):
+    return lax.dot_general(a, b, (((1,), (1,)), ((), ())), preferred_element_type=F32)
+
+
+def tn(a, b):
+    return lax.dot_general(a, b, (((0,), (0,)), ((), ())), preferred_element_type=F32)
+
+
+def cat(ref):
+    return jnp.concatenate([ref[i] for i in range(ref.shape[0])], axis=1)
+
+
+def put(ref, values):
+    width = ref.shape[-1]
+    for i in range(ref.shape[0]):
+        ref[i] = values[:, i * width : (i + 1) * width].astype(ref.dtype)
+
+
+def centred(values):
+    centre = values - jnp.mean(values, axis=0, keepdims=True)
+    rstd = lax.rsqrt(jnp.mean(centre * centre, axis=0, keepdims=True) + EPS)
+    return centre * rstd, rstd
+
+
+def norm_back(values, gain, grad, sums):
+    hat, rstd = centred(values)
+    scaled = grad * hat
+    for k in range(values.shape[1] // 128):
+        sums[0] += scaled[:, k * 128 : (k + 1) * 128]
+        sums[1] += grad[:, k * 128 : (k + 1) * 128]
+    inner = grad * gain
+    return rstd * (
+        inner
+        - jnp.mean(inner, axis=0, keepdims=True)
+        - hat * jnp.mean(inner * hat, axis=0, keepdims=True)
+    )
+
+
+def put_sums(ref, sums):
+    ref[0:1, :] = jnp.sum(sums[0].T, axis=0, keepdims=True)
+    ref[1:2, :] = jnp.sum(sums[1].T, axis=0, keepdims=True)
+
+
+def gelu_pair(u):
+    c0, c1 = 0.7978845608028654, 0.044715
+    square = u * u
+    tanh = jnp.tanh(u * (c0 + (c0 * c1) * square))
+    half = 0.5 + 0.5 * tanh
+    slope = half + (0.5 * u) * (1.0 - tanh * tanh) * (c0 + (3 * c0 * c1) * square)
+    return u * half, slope
+
+
+def quarter(place, index):
+    return (place[0] ^ (index // 2)) * 2 + (place[1] ^ (index % 2))
+
+
+def weight_copies(place, layer, by_rows, mine, pieces, held, sem):
+    rows, cols = mine.shape[1], mine.shape[2]
+    part = rows // 4
+    if by_rows:
+        copies = [pltpu.make_async_copy(mine.at[layer], held.at[0:rows, :], sem.at[0])]
+    else:
+        copies = [pltpu.make_async_copy(mine.at[layer], held.at[:, 0:cols], sem.at[0])]
+    for index, piece in enumerate(pieces):
+        if by_rows:
+            start = pl.multiple_of(rows + quarter(place, index) * part, part)
+            target = held.at[pl.ds(start, part), :]
+        else:
+            start = pl.multiple_of(quarter(place, index) * part, part)
+            target = held.at[pl.ds(start, part), cols : 2 * cols]
+        copies.append(pltpu.make_async_copy(piece, target, sem.at[1 + index]))
+    return copies
+
+
+def put_grads(place, by_rows, total, keep, send):
+    part, cols = keep.shape[2], keep.shape[3]
+    for dx in range(2):
+        for index in range(4):
+            start = quarter(place, index) * part
+            if by_rows:
+                start = pl.multiple_of(dx * 4 * part + start, part)
+                values = total[pl.ds(start, part), :]
+            else:
+                start = pl.multiple_of(start, part)
+                values = total[pl.ds(start, part), dx * cols : (dx + 1) * cols]
+            target = send if index % 2 else keep
+            target[dx, index // 2] = values.astype(BF)
+
+
+def spatial_forward_kernel(
+    layer, place, x_ref, bias_ref, norm_ref, wq, q0, q1, q2, q3, wo, o0, o1, o2, o3,
+    p_ref, o_ref, r_ref, a2_ref, stat_ref, wq_v, wo_v, sem_q, sem_o,
+):
+    @pl.when(pl.program_id(0) == 0)
+    def _():
+        copies = weight_copies(place, layer, False, wq, (q0, q1, q2, q3), wq_v, sem_q)
+        copies += weight_copies(place, layer, True, wo, (o0, o1, o2, o3), wo_v, sem_o)
+        for copy in copies:
+            copy.start()
+        for copy in copies:
+            copy.wait()
+
+    x = x_ref[...].astype(F32).T
+    hat, _ = centred(x)
+    a = (hat * norm_ref[:, 0:1] + norm_ref[:, 1:2]).astype(BF)
+    put(p_ref, tn(wq_v[...], a))
+    heads = wq_v.shape[1] // (3 * HEAD_DIM)
+    for frame in range(p_ref.shape[0]):
+        bias = bias_ref[0]
+
+        def one_head(h, _):
+            base = pl.multiple_of(h * 3 * HEAD_DIM, HEAD_DIM)
+            q = p_ref[frame, pl.ds(base, HEAD_DIM), :] * SCALE
+            k = p_ref[frame, pl.ds(base + HEAD_DIM, HEAD_DIM), :]
+            v = p_ref[frame, pl.ds(base + 2 * HEAD_DIM, HEAD_DIM), :]
+            s = tn(k, q.astype(BF)) + bias
+            top = jnp.max(s, axis=0, keepdims=True)
+            e = jnp.exp(s - top)
+            inverse = 1.0 / jnp.sum(e, axis=0, keepdims=True)
+            stat_ref[frame, pl.ds(h, 1), :] = top
+            stat_ref[frame, pl.ds(heads + h, 1), :] = inverse
+            o = nn(v, (e * inverse).astype(BF))
+            o_ref[frame, pl.ds(pl.multiple_of(h * HEAD_DIM, HEAD_DIM), HEAD_DIM), :] = (
+                o.astype(BF)
+            )
+            return 0
+
+        lax.fori_loop(0, heads, one_head, 0, unroll=2)
+    r = x + tn(wo_v[...], cat(o_ref))
+    put(r_ref, r)
+    hat, _ = centred(r)
+    put(a2_ref, hat * norm_ref[:, 2:3] + norm_ref[:, 3:4])
+
+
+def mlp_forward_kernel(
+    layer, chunk, place, r_ref, a2_ref, wu, u0, u1, u2, u3, wd, d0, d1, d2, d3,
+    x_ref, g_ref, slope_ref, total, wu_v, wd_v, sem_u, sem_d,
+):
+    @pl.when(pl.program_id(0) == 0)
+    def _():
+        copies = weight_copies(place, layer, False, wu, (u0, u1, u2, u3), wu_v, sem_u)
+        copies += weight_copies(place, layer, True, wd, (d0, d1, d2, d3), wd_v, sem_d)
+        for copy in copies:
+            copy.start()
+        for copy in copies:
+            copy.wait()
+
+    a2 = cat(a2_ref)
+    total[...] = cat(r_ref)
+
+    def step(j, _):
+        for part in range(2):
+            here = pl.ds(pl.multiple_of((2 * j + part) * chunk, chunk), chunk)
+            g, slope = gelu_pair(tn(wu_v[:, here], a2))
+            g = g.astype(BF)
+            g_ref[0, here, :] = g
+            slope_ref[0, here, :] = slope.astype(BF)
+            total[...] += tn(wd_v[here, :], g)
+        return 0
+
+    lax.fori_loop(0, wu_v.shape[1] // (2 * chunk), step, 0)
+    put(x_ref, total[...])
+
+
+def temporal_weights(p_ref, h, clip_ref, stream):
+    base = pl.multiple_of(h * 3 * HEAD_DIM, HEAD_DIM)
+    take = lambda f, c: p_ref[f, pl.ds(base + c * HEAD_DIM, HEAD_DIM), :].astype(F32)
+    q = [take(f, 0) for f in range(FRAMES)]
+    k = [take(f, 1) for f in range(FRAMES)]
+    v = [take(f, 2) for f in range(FRAMES)]
+    weights = []
+    for f in range(FRAMES):
+        scores = []
+        for g in range(f + 1):
+            bias = jnp.where(clip_ref[stream, g] == clip_ref[stream, f], 0.0, -1000000000.0)
+            scores.append(jnp.sum(q[f] * k[g], axis=0, keepdims=True) * SCALE + bias)
+        top = functools.reduce(jnp.maximum, scores)
+        e = [jnp.exp(s - top) for s in scores]
+        inverse = 1.0 / functools.reduce(jnp.add, e)
+        weights.append([x * inverse for x in e])
+    return q, k, v, weights
+
+
+def low(v):
+    return v.astype(BF).astype(F32)
+
+
+def temporal_forward_kernel(
+    layer, place, clip_ref, x_ref, norm_ref, wq, q0, q1, q2, q3, wo, o0, o1, o2, o3,
+    p_ref, o_ref, r_ref, a2_ref, wq_v, wo_v, sem_q, sem_o,
+):
+    @pl.when((pl.program_id(0) == 0) & (pl.program_id(1) == 0))
+    def _():
+        copies = weight_copies(place, layer, False, wq, (q0, q1, q2, q3), wq_v, sem_q)
+        copies += weight_copies(place, layer, True, wo, (o0, o1, o2, o3), wo_v, sem_o)
+        for copy in copies:
+            copy.start()
+        for copy in copies:
+            copy.wait()
+
+    stream = pl.program_id(0)
+    x = cat(x_ref)
+    hat, _ = centred(x)
+    a = (hat * norm_ref[:, 4:5] + norm_ref[:, 5:6]).astype(BF)
+    put(p_ref, tn(wq_v[...], a))
+    heads = wq_v.shape[1] // (3 * HEAD_DIM)
+
+    def one_head(h, _):
+        _, _, v, weights = temporal_weights(p_ref, h, clip_ref, stream)
+        rows = pl.ds(pl.multiple_of(h * HEAD_DIM, HEAD_DIM), HEAD_DIM)
+        for f in range(FRAMES):
+            o = functools.reduce(jnp.add, [low(w) * v[g] for g, w in enumerate(weights[f])])
+            o_ref[f, rows, :] = o.astype(BF)
+        return 0
+
+    lax.fori_loop(0, heads, one_head, 0)
+    r = x + tn(wo_v[...], cat(o_ref))
+    put(r_ref, r)
+    hat, _ = centred(r)
+    put(a2_ref, hat * norm_ref[:, 6:7] + norm_ref[:, 7:8])
+
+
+def mlp_both_kernel(
+    layer, chunk, place, r_ref, a2_ref, y_ref, norm_ref, wu, u0, u1, u2, u3, wd, d0, d1, d2, d3,
+    out_ref, dr_ref, ku_ref, su_ref, kd_ref, sd_ref, ln_ref,
+    total, back, gu, gd, sums, wu_v, wd_v, sem_u, sem_d,
+):
+    @pl.when(pl.program_id(0) == 0)
+    def _():
+        copies = weight_copies(place, layer, False, wu, (u0, u1, u2, u3), wu_v, sem_u)
+        copies += weight_copies(place, layer, True, wd, (d0, d1, d2, d3), wd_v, sem_d)
+        for copy in copies:
+            copy.start()
+        gu[...] = jnp.zeros_like(gu)
+        gd[...] = jnp.zeros_like(gd)
+        sums[...] = jnp.zeros_like(sums)
+        for copy in copies:
+            copy.wait()
+
+    a2 = cat(a2_ref)
+    dm = y_ref[...].T
+    total[...] = cat(r_ref)
+    back[...] = jnp.zeros_like(back)
+
+    def step(j, _):
+        for part in range(2):
+            here = pl.ds(pl.multiple_of((2 * j + part) * chunk, chunk), chunk)
+            g, slope = gelu_pair(tn(wu_v[:, here], a2))
+            g = g.astype(BF)
+            du = (nn(wd_v[here, :], dm) * slope).astype(BF)
+            total[...] += tn(wd_v[here, :], g)
+            gd[here, :] += nt(g, dm)
+            gu[:, here] += nt(a2, du)
+            back[...] += nn(wu_v[:, here], du)
+        return 0
+
+    lax.fori_loop(0, wu_v.shape[1] // (2 * chunk), step, 0)
+    out_ref[...] = total[...].astype(BF).T
+    put(dr_ref, dm.astype(F32) + norm_back(cat(r_ref), norm_ref[:, 6:7], back[...], sums))
+
+    @pl.when(pl.program_id(0) == pl.num_programs(0) - 1)
+    def _():
+        put_grads(place, False, gu, ku_ref, su_ref)
+        put_grads(place, True, gd, kd_ref, sd_ref)
+        put_sums(ln_ref, sums)
+
+
+def mlp_back_kernel(
+    layer, chunk, place, r_ref, a2_ref, y_ref, g_ref, slope_ref, norm_ref,
+    wu, u0, u1, u2, u3, wd, d0, d1, d2, d3,
+    dr_ref, ku_ref, su_ref, kd_ref, sd_ref, ln_ref,
+    back, gu, gd, sums, wu_v, wd_v, sem_u, sem_d,
+):
+    @pl.when(pl.program_id(0) == 0)
+    def _():
+        copies = weight_copies(place, layer, False, wu, (u0, u1, u2, u3), wu_v, sem_u)
+        copies += weight_copies(place, layer, True, wd, (d0, d1, d2, d3), wd_v, sem_d)
+        for copy in copies:
+            copy.start()
+        gu[...] = jnp.zeros_like(gu)
+        gd[...] = jnp.zeros_like(gd)
+        sums[...] = jnp.zeros_like(sums)
+        for copy in copies:
+            copy.wait()
+
+    a2 = cat(a2_ref)
+    dm = cat(y_ref).astype(BF)
+    back[...] = jnp.zeros_like(back)
+
+    def step(j, _):
+        for part in range(2):
+            here = pl.ds(pl.multiple_of((2 * j + part) * chunk, chunk), chunk)
+            du = (nn(wd_v[here, :], dm) * slope_ref[0, here, :].astype(F32)).astype(BF)
+            gd[here, :] += nt(g_ref[0, here, :], dm)
+            gu[:, here] += nt(a2, du)
+            back[...] += nn(wu_v[:, here], du)
+        return 0
+
+    lax.fori_loop(0, wu_v.shape[1] // (2 * chunk), step, 0)
+    put(dr_ref, cat(y_ref) + norm_back(cat(r_ref), norm_ref[:, 2:3], back[...], sums))
+
+    @pl.when(pl.program_id(0) == pl.num_programs(0) - 1)
+    def _():
+        put_grads(place, False, gu, ku_ref, su_ref)
+        put_grads(place, True, gd, kd_ref, sd_ref)
+        put_sums(ln_ref, sums)
+
+
+def temporal_back_kernel(
+    layer, place, clip_ref, x_ref, y_ref, p_ref, o_ref, norm_ref,
+    wq, q0, q1, q2, q3, wo, o0, o1, o2, o3,
+    dx_ref, kq_ref, sq_ref, ko_ref, so_ref, ln_ref,
+    gq, go, sums, do_v, dp_v, wq_v, wo_v, sem_q, sem_o,
+):
+    first = (pl.program_id(0) == 0) & (pl.program_id(1) == 0)
+    last = (pl.program_id(0) == pl.num_programs(0) - 1) & (
+        pl.program_id(1) == pl.num_programs(1) - 1
+    )
+
+    @pl.when(first)
+    def _():
+        copies = weight_copies(place, layer, False, wq, (q0, q1, q2, q3), wq_v, sem_q)
+        copies += weight_copies(place, layer, True, wo, (o0, o1, o2, o3), wo_v, sem_o)
+        for copy in copies:
+            copy.start()
+        gq[...] = jnp.zeros_like(gq)
+        go[...] = jnp.zeros_like(go)
+        sums[...] = jnp.zeros_like(sums)
+        for copy in copies:
+            copy.wait()
+
+    stream = pl.program_id(0)
+    da = cat(y_ref).astype(BF)
+    go[...] += nt(cat(o_ref), da)
+    put(do_v, nn(wo_v[...], da))
+    heads = wq_v.shape[1] // (3 * HEAD_DIM)
+
+    def one_head(h, _):
+        q, k, v, weights = temporal_weights(p_ref, h, clip_ref, stream)
+        base = pl.multiple_of(h * 3 * HEAD_DIM, HEAD_DIM)
+        rows = pl.ds(pl.multiple_of(h * HEAD_DIM, HEAD_DIM), HEAD_DIM)
+        do = [do_v[f, rows, :].astype(F32) for f in range(FRAMES)]
+        dk = [0.0] * FRAMES
+        dv = [0.0] * FRAMES
+        for f in range(FRAMES):
+            dw = [jnp.sum(do[f] * v[g], axis=0, keepdims=True) for g in range(f + 1)]
+            inner = functools.reduce(jnp.add, [w * d for w, d in zip(weights[f], dw)])
+            dq = 0.0
+            for g in range(f + 1):
+                ds = low(weights[f][g] * (dw[g] - inner)) * SCALE
+                dq = dq + ds * k[g]
+                dk[g] = dk[g] + ds * q[f]
+                dv[g] = dv[g] + low(weights[f][g]) * do[f]
+            dp_v[f, pl.ds(base, HEAD_DIM), :] = dq.astype(BF)
+        for g in range(FRAMES):
+            dp_v[g, pl.ds(base + HEAD_DIM, HEAD_DIM), :] = dk[g].astype(BF)
+            dp_v[g, pl.ds(base + 2 * HEAD_DIM, HEAD_DIM), :] = dv[g].astype(BF)
+        return 0
+
+    lax.fori_loop(0, heads, one_head, 0)
+    x = cat(x_ref)
+    hat, _ = centred(x)
+    a = (hat * norm_ref[:, 4:5] + norm_ref[:, 5:6]).astype(BF)
+    dp = cat(dp_v)
+    gq[...] += nt(a, dp)
+    put(dx_ref, cat(y_ref) + norm_back(x, norm_ref[:, 4:5], nn(wq_v[...], dp), sums))
+
+    @pl.when(last)
+    def _():
+        put_grads(place, False, gq, kq_ref, sq_ref)
+        put_grads(place, True, go, ko_ref, so_ref)
+        put_sums(ln_ref, sums)
+
+
+def spatial_back_kernel(
+    layer, place, x_ref, bias_ref, y_ref, p_ref, o_ref, stat_ref, norm_ref,
+    wq, q0, q1, q2, q3, wo, o0, o1, o2, o3,
+    dx_ref, kq_ref, sq_ref, ko_ref, so_ref, ln_ref,
+    gq, go, sums, do_v, dp_v, wq_v, wo_v, sem_q, sem_o,
+):
+    @pl.when(pl.program_id(0) == 0)
+    def _():
+        copies = weight_copies(place, layer, False, wq, (q0, q1, q2, q3), wq_v, sem_q)
+        copies += weight_copies(place, layer, True, wo, (o0, o1, o2, o3), wo_v, sem_o)
+        for copy in copies:
+            copy.start()
+        gq[...] = jnp.zeros_like(gq)
+        go[...] = jnp.zeros_like(go)
+        sums[...] = jnp.zeros_like(sums)
+        for copy in copies:
+            copy.wait()
+
+    da = cat(y_ref).astype(BF)
+    go[...] += nt(cat(o_ref), da)
+    put(do_v, nn(wo_v[...], da))
+    heads = wq_v.shape[1] // (3 * HEAD_DIM)
+    for frame in range(p_ref.shape[0]):
+        bias = bias_ref[0]
+
+        def one_head(h, _):
+            base = pl.multiple_of(h * 3 * HEAD_DIM, HEAD_DIM)
+            q = (p_ref[frame, pl.ds(base, HEAD_DIM), :] * SCALE).astype(BF)
+            k = p_ref[frame, pl.ds(base + HEAD_DIM, HEAD_DIM), :]
+            v = p_ref[frame, pl.ds(base + 2 * HEAD_DIM, HEAD_DIM), :]
+            do = do_v[frame, pl.ds(pl.multiple_of(h * HEAD_DIM, HEAD_DIM), HEAD_DIM), :]
+            top = stat_ref[frame, pl.ds(h, 1), :]
+            inverse = stat_ref[frame, pl.ds(heads + h, 1), :]
+            w = jnp.exp(tn(k, q) + bias - top) * inverse
+            dw = tn(v, do)
+            inner = jnp.sum(w * dw, axis=0, keepdims=True)
+            ds = (w * (dw - inner)).astype(BF)
+            dq = nn(k, ds) * SCALE
+            dp_v[frame, pl.ds(base, HEAD_DIM), :] = dq.astype(BF)
+            dp_v[frame, pl.ds(base + HEAD_DIM, HEAD_DIM), :] = nt(q, ds).astype(BF)
+            dp_v[frame, pl.ds(base + 2 * HEAD_DIM, HEAD_DIM), :] = nt(do, w.astype(BF)).astype(BF)
+            return 0
+
+        lax.fori_loop(0, heads, one_head, 0, unroll=2)
+    x = x_ref[...].astype(F32).T
+    hat, _ = centred(x)
+    a = (hat * norm_ref[:, 0:1] + norm_ref[:, 1:2]).astype(BF)
+    dp = cat(dp_v)
+    gq[...] += nt(a, dp)
+    dx = cat(y_ref) + norm_back(x, norm_ref[:, 0:1], nn(wq_v[...], dp), sums)
+    dx_ref[...] = dx.T
+
+    @pl.when(pl.program_id(0) == pl.num_programs(0) - 1)
+    def _():
+        put_grads(place, False, gq, kq_ref, sq_ref)
+        put_grads(place, True, go, ko_ref, so_ref)
+        put_sums(ln_ref, sums)
+
+
+ANY = pl.BlockSpec(memory_space=pl.ANY)
+SMEM = pl.BlockSpec(memory_space=pltpu.SMEM)
+
+
+def whole(shape):
+    zeros = (0,) * len(shape)
+    return pl.BlockSpec(shape, lambda *_: zeros, pipeline_mode=pl.Buffered(1))
+
+
+def call(body, name, grid, ins, outs, scratch, cost):
+    flops, exps = cost
+    moved = sum(a.size * a.dtype.itemsize for a, _ in ins)
+    shapes = [jax.ShapeDtypeStruct(shape, dtype) for shape, dtype, _ in outs]
+    moved += sum(s.size * s.dtype.itemsize for s in shapes)
+    return pl.pallas_call(
+        body,
+        grid=grid,
+        in_specs=[spec for _, spec in ins],
+        out_specs=[spec for _, _, spec in outs],
+        out_shape=shapes,
+        scratch_shapes=scratch,
+        compiler_params=pltpu.CompilerParams(
+            vmem_limit_bytes=VMEM_BYTES, dimension_semantics=("arbitrary",) * len(grid)
+        ),
+        cost_estimate=pl.CostEstimate(
+            flops=int(flops), transcendentals=int(exps), bytes_accessed=int(moved)
+        ),
+        name=name,
+    )(*[a for a, _ in ins])
+
+
+def weight_ins(mine, pieces):
+    return [(mine, ANY)] + [(piece, ANY) for piece in pieces]
+
+
+def held(mine, by_rows):
+    rows, cols = mine.shape[1:]
+    return pltpu.VMEM((2 * rows, cols) if by_rows else (rows, 2 * cols), BF)
+
+
+def held_grad(mine, by_rows):
+    rows, cols = mine.shape[1:]
+    return pltpu.VMEM((2 * rows, cols) if by_rows else (rows, 2 * cols), F32)
+
+
+def grad_outs(mine):
+    shape = (2, 2, mine.shape[1] // 4, mine.shape[2])
+    return [(shape, BF, whole(shape))] * 2
+
+
+SEMS = pltpu.SemaphoreType.DMA((5,))
+
+
+def fetch(weight, layer, place):
+    part = weight.shape[1] // 4
+    start = (place[0] * 2 + place[1]) * part
+    own = lax.dynamic_slice(weight, (layer, start, 0), (1, part, weight.shape[2]))[0]
+    near = lax.ppermute(own, "mp", SWAP)
+    side = lax.ppermute(near, "y", SWAP)
+    return (
+        near,
+        lax.ppermute(near, "core", SWAP),
+        side,
+        lax.ppermute(side, "core", SWAP),
+    )
+
+
+def add(a, b):
+    return (a.astype(F32) + b.astype(F32)).astype(a.dtype)
+
+
+def over_z(value, z):
+    inward = add(value, lax.ppermute(value, "z", [(0, 1), (3, 2)]))
+    middle = add(inward, lax.ppermute(inward, "z", [(1, 2), (2, 1)]))
+    outward = lax.ppermute(middle, "z", [(1, 0), (2, 3)])
+    return jnp.where((z == 1) | (z == 2), middle, outward)
+
+
+def reduce(keep, send, z):
+    got = lax.ppermute(send, "core", SWAP)
+    far = add(keep[1], got[1])
+    near = (keep[0].astype(F32) + got[0].astype(F32)).astype(BF)
+    near = add(near, lax.ppermute(far, "mp", SWAP))
+    mine = over_z(add(near[0], lax.ppermute(near[1], "y", SWAP)), z)
+    side = lax.ppermute(mine, "y", SWAP)
+    return (mine, lax.ppermute(mine, "core", SWAP), side, lax.ppermute(side, "core", SWAP))
+
+
+def reduce_small(value, z):
+    for axis in ("core", "mp", "y"):
+        value = value + lax.ppermute(value, axis, SWAP)
+    return over_z(value, z)
+
+
+def finish_kernel(place, *refs):
+    pieces, outs = refs[:-2], refs[-2:]
+    for t, out in enumerate(outs):
+        part = out.shape[1] // 4
+        for layer in range(2):
+            for index in range(4):
+                start = pl.multiple_of(quarter(place, index) * part, part)
+                piece = pieces[t * 8 + layer * 4 + index]
+                out[layer, pl.ds(start, part), :] = piece[...].astype(F32)
+
+
+def finish(place, first, second, shapes):
+    pieces = [p for pair in (first, second) for layer in pair for p in layer]
+    ins = [(place, SMEM)] + [(p, whole(p.shape)) for p in pieces]
+    outs = [(s, F32, whole(s)) for s in shapes]
+    return call(finish_kernel, "finish", (1,), ins, outs, [], (0, 0))
+
+
+def shards(tokens, out_grad, patch_valid, clip_ids, ln_gain, ln_bias, w_qkv, w_out, w_up, w_down):
+    z, y, core, mp = (lax.axis_index(a) for a in ("z", "y", "core", "mp"))
+    place = jnp.stack([y, core]).astype(jnp.int32)
+    n, width = tokens.shape
+    patches = patch_valid.shape[1]
+    frames = n // patches
+    streams = frames // FRAMES
+    hidden = 2 * w_up.shape[2]
+    heads = 2 * w_qkv.shape[2] // (3 * HEAD_DIM)
+    qkv = 2 * w_qkv.shape[2]
+    inner = 2 * w_out.shape[1]
+
+    valid = lax.dynamic_slice(patch_valid, (mp * streams, 0), (streams, patches))
+    bias = jnp.where(valid == 1, 0.0, -1000000000.0).astype(F32)[:, :, None]
+    clips = lax.dynamic_slice(clip_ids, (mp * streams, 0), (streams, FRAMES))
+    norms = jnp.stack([ln_gain, ln_bias], axis=2).reshape(8, width).T
+
+    got = {}
+    for layer in range(2):
+        for name, weight in (("qkv", w_qkv), ("out", w_out), ("up", w_up), ("down", w_down)):
+            got[name, layer] = fetch(weight, layer, (y, core))
+
+    def attn_ins(layer):
+        return weight_ins(w_qkv, got["qkv", layer]) + weight_ins(w_out, got["out", layer])
+
+    def mlp_ins(layer):
+        return weight_ins(w_up, got["up", layer]) + weight_ins(w_down, got["down", layer])
+
+    attn_held = [held(w_qkv, False), held(w_out, True), SEMS, SEMS]
+    mlp_held = [held(w_up, False), held(w_down, True), SEMS, SEMS]
+    norm_in = (norms, whole(norms.shape))
+    place_in = (place, SMEM)
+    both = 2 if frames % 2 == 0 else 1
+    span = both * patches
+    tiles = frames // both
+    chunk = min(512, hidden // 2)
+
+    def rows(count, features):
+        return pl.BlockSpec((count, features, patches), lambda i: (i, 0, 0))
+
+    def columns(width_):
+        return pl.BlockSpec((FRAMES, width_, 128), lambda i, j: (i, 0, j))
+
+    token_rows = lambda count: pl.BlockSpec((count * patches, width), lambda i: (i, 0))
+    act = lambda features: (frames, features, patches)
+    bias_of = lambda count: pl.BlockSpec(
+        (1, patches, 1), lambda i: (i * count // FRAMES, 0, 0)
+    )
+    ln_out = ((8, width), F32, whole((8, width)))
+    spatial_flops = 4 * n * patches * inner
+    attn_flops = 2 * n * width * (qkv + inner)
+    mlp_flops = 4 * n * width * hidden
+
+    p0, o0, r0, a0, stat0 = call(
+        functools.partial(spatial_forward_kernel, 0), "spatial_forward", (tiles,),
+        [place_in, (tokens, token_rows(both)), (bias, bias_of(both)), norm_in] + attn_ins(0),
+        [(act(qkv), BF, rows(both, qkv)), (act(inner), BF, rows(both, inner)),
+         (act(width), F32, rows(both, width)), (act(width), BF, rows(both, width)),
+         (act(2 * heads), F32, rows(both, 2 * heads))],
+        attn_held, (attn_flops + spatial_flops, n * patches * heads),
+    )
+    saved = (tiles, hidden, span)
+    saved_spec = pl.BlockSpec((1, hidden, span), lambda i: (i, 0, 0))
+    x1, g0, slope0 = call(
+        functools.partial(mlp_forward_kernel, 0, chunk), "mlp_forward", (tiles,),
+        [place_in, (r0, rows(both, width)), (a0, rows(both, width))] + mlp_ins(0),
+        [(act(width), F32, rows(both, width)), (saved, BF, saved_spec), (saved, BF, saved_spec)],
+        [pltpu.VMEM((width, span), F32)] + mlp_held, (mlp_flops, n * hidden),
+    )
+
+    clip_in = (clips, SMEM)
+    grid1 = (streams, patches // 128)
+    p1, o1, r1, a1 = call(
+        functools.partial(temporal_forward_kernel, 1), "temporal_forward", grid1,
+        [place_in, clip_in, (x1, columns(width)), norm_in] + attn_ins(1),
+        [(act(qkv), BF, columns(qkv)), (act(inner), BF, columns(inner)),
+         (act(width), F32, columns(width)), (act(width), BF, columns(width))],
+        attn_held, (attn_flops * 1.2, 0),
+    )
+    layer_out, dr1, ku1, su1, kd1, sd1, ln11 = call(
+        functools.partial(mlp_both_kernel, 1, chunk), "mlp_both", (tiles,),
+        [place_in, (r1, rows(both, width)), (a1, rows(both, width)),
+         (out_grad, token_rows(both)), norm_in] + mlp_ins(1),
+        [((n, width), BF, token_rows(both)), (act(width), F32, rows(both, width))]
+        + grad_outs(w_up) + grad_outs(w_down) + [ln_out],
+        [pltpu.VMEM((width, span), F32), pltpu.VMEM((width, span), F32),
+         held_grad(w_up, False), held_grad(w_down, True), pltpu.VMEM((2, width, 128), F32)]
+        + mlp_held,
+        (3 * mlp_flops, n * hidden),
+    )
+    up1 = reduce(ku1, su1, z)
+    down1 = reduce(kd1, sd1, z)
+    dx1, kq1, sq1, ko1, so1, ln10 = call(
+        functools.partial(temporal_back_kernel, 1), "temporal_back", grid1,
+        [place_in, clip_in, (x1, columns(width)), (dr1, columns(width)), (p1, columns(qkv)),
+         (o1, columns(inner)), norm_in] + attn_ins(1),
+        [(act(width), F32, columns(width))] + grad_outs(w_qkv) + grad_outs(w_out) + [ln_out],
+        [held_grad(w_qkv, False), held_grad(w_out, True), pltpu.VMEM((2, width, 128), F32),
+         pltpu.VMEM((FRAMES, inner, 128), BF), pltpu.VMEM((FRAMES, qkv, 128), BF)] + attn_held,
+        (2.4 * attn_flops, 0),
+    )
+    qkv1 = reduce(kq1, sq1, z)
+    out1 = reduce(ko1, so1, z)
+
+    dr0, ku0, su0, kd0, sd0, ln01 = call(
+        functools.partial(mlp_back_kernel, 0, chunk), "mlp_back", (tiles,),
+        [place_in, (r0, rows(both, width)), (a0, rows(both, width)), (dx1, rows(both, width)),
+         (g0, saved_spec), (slope0, saved_spec), norm_in] + mlp_ins(0),
+        [(act(width), F32, rows(both, width))] + grad_outs(w_up) + grad_outs(w_down) + [ln_out],
+        [pltpu.VMEM((width, span), F32), held_grad(w_up, False), held_grad(w_down, True),
+         pltpu.VMEM((2, width, 128), F32)] + mlp_held,
+        (2 * mlp_flops, 0),
+    )
+    up0 = reduce(ku0, su0, z)
+    down0 = reduce(kd0, sd0, z)
+    input_grad, kq0, sq0, ko0, so0, ln00 = call(
+        functools.partial(spatial_back_kernel, 0), "spatial_back", (tiles,),
+        [place_in, (tokens, token_rows(both)), (bias, bias_of(both)), (dr0, rows(both, width)),
+         (p0, rows(both, qkv)), (o0, rows(both, inner)), (stat0, rows(both, 2 * heads)),
+         norm_in] + attn_ins(0),
+        [((n, width), F32, token_rows(both))] + grad_outs(w_qkv) + grad_outs(w_out) + [ln_out],
+        [held_grad(w_qkv, False), held_grad(w_out, True), pltpu.VMEM((2, width, 128), F32),
+         pltpu.VMEM((both, inner, patches), BF), pltpu.VMEM((both, qkv, patches), BF)]
+        + attn_held,
+        (2 * attn_flops + 2.5 * spatial_flops, n * patches * heads),
+    )
+    qkv0 = reduce(kq0, sq0, z)
+    out0 = reduce(ko0, so0, z)
+
+    small = reduce_small(jnp.stack([ln00[:2], ln01[:2], ln10[:2], ln11[:2]]), z)
+    small = small.reshape(2, 2, 2, width)
+    grad_up, grad_down = finish(place, (up0, up1), (down0, down1), (w_up.shape, w_down.shape))
+    grad_qkv, grad_out = finish(place, (qkv0, qkv1), (out0, out1), (w_qkv.shape, w_out.shape))
+    return (
+        layer_out,
+        input_grad,
+        small[:, :, 0],
+        small[:, :, 1],
+        grad_qkv,
+        grad_out,
+        grad_up,
+        grad_down,
+    )
 
 
 SPATIAL_FORMS = ("sfphe,sfqhe->sfhpq", "sfhpq,sfqhe->sfphe", "sfhpq,sfphe->sfqhe")
@@ -214,7 +919,7 @@
     )
 
 
-def shards(tokens, out_grad, patch_valid, clip_ids, ln_gain, ln_bias, w_qkv, w_out, w_up, w_down):
+def split_shards(tokens, out_grad, patch_valid, clip_ids, ln_gain, ln_bias, w_qkv, w_out, w_up, w_down):
     streams = patch_valid.shape[0]
     space_bias, time_bias = mask_biases(patch_valid, clip_ids)
     up_use, down_use = (w_up, w_down)
@@ -286,30 +991,39 @@
 
 
 def solution(mesh):
+    dp, mp = mesh.shape["dp"], mesh.shape["mp"]
+    if (dp, mp) != (16, 2):
+        return on_mesh(split_shards, mesh, ("dp",), "mp")
+    fine = Mesh(mesh.devices.reshape(4, 2, 2, 2), ("z", "y", "core", "mp"))
+    return on_mesh(shards, fine, ("z", "y", "core"), "mp")
+
+
+def on_mesh(body, mesh, dp, mp):
+    both = dp + (mp,)
     return jax.shard_map(
-        shards,
+        body,
         mesh=mesh,
         in_specs=(
-            P(("dp", "mp"), None),
-            P(("dp", "mp"), None),
-            P("dp", None),
-            P("dp", None),
+            P(both, None),
+            P(both, None),
+            P(dp, None),
+            P(dp, None),
             P(),
             P(),
-            P(None, None, "mp"),
-            P(None, "mp", None),
-            P(None, None, "mp"),
-            P(None, "mp", None),
+            P(None, None, mp),
+            P(None, mp, None),
+            P(None, None, mp),
+            P(None, mp, None),
         ),
         out_specs=(
-            P(("dp", "mp"), None),
-            P(("dp", "mp"), None),
+            P(both, None),
+            P(both, None),
             P(),
             P(),
-            P(None, None, "mp"),
-            P(None, "mp", None),
-            P(None, None, "mp"),
-            P(None, "mp", None),
+            P(None, None, mp),
+            P(None, mp, None),
+            P(None, None, mp),
+            P(None, mp, None),
         ),
         check_vma=False,
     )

time: 1640 us -> 576 us (0.35)
  waiting for transfers between devices: 937 us -> 186 us
  matrix products: 302 us -> 0 us
  Pallas kernels: 0 us -> 244 us
  local copies, waits for them, and re-layouts: 187 us -> 14.3 us
  other arithmetic: 151 us -> 6.19 us
  starting transfers between devices: 1.11 us -> 113 us
  blocking collectives: 39.5 us -> 0 us
    all_gather x8 -> x0, waiting for transfers between devices: 411 us -> none  [the longest x4 217 us: norm_gather(): return lax.all_gather(normed, 'mp', axis=0, tiled=True)]
    reduce_scatter x8 -> x0, waiting for transfers between devices: 394 us -> none  [the longest x4 214 us: branch_scatter(): lax.psum_scatter(jnp.dot(values_bf, weight, preferred_element_type=jnp.fl...]
    dot_general x36 -> x0, matrix products: 302 us -> none  [the longest x2 33.1 us: block_forward(): hidden_pre = jnp.dot(second_full, w_up, preferred_element_type=jnp.float32)]
    pallas_call x0 -> x9, Pallas kernels: none -> 244 us  [call(): pl.pallas_call(body, grid=grid, in_specs=[spec for _, spec in ins], out_s...]
    ppermute x0 -> x110, waiting for transfers between devices: none -> 186 us  [the longest x9 54.6 us: over_z(): outward = lax.ppermute(middle, 'z', [(1, 0), (2, 3)])]
    psum x1 -> x0, waiting for transfers between devices: 132 us -> none  [shards(): lax.psum(stacked[0].astype(jnp.bfloat16), 'dp').astype(jnp.float32)]
    ppermute x0 -> x110, starting transfers between devices: none -> 113 us  [the longest x9 38.3 us: over_z(): inward = add(value, lax.ppermute(value, 'z', [(0, 1), (3, 2)]))]
    reshape x9 -> x2, local copies, waits for them, and re-layouts: 73.3 us -> 0.85 us  [shards(): norms = jnp.stack([ln_gain, ln_bias], axis=2).reshape(8, width).T]
  transfers between devices with their start and end apart: 17 -> 110, of which waited for: 17 -> 45; matrix products, arithmetic and copies ran while one was open for 6% -> 2% of each run, Pallas kernels for 0% -> 15%
where the time goes in v1:
time: 576 us; the launch traced here: 566 us
  Pallas kernels  244 us (42%)
  waiting for transfers between devices  186 us (32%)
  starting transfers between devices  113 us (20%)
  local copies, waits for them, and re-layouts  14.3 us (2%)
  other arithmetic  6.19 us (1%)
    pallas_call x9, Pallas kernels, call(): pl.pallas_call(body, grid=grid, in_specs=[spec for _, spec in ins], out_s...  244 us
    ppermute x9, waiting for transfers between devices, over_z(): outward = lax.ppermute(middle, 'z', [(1, 0), (2, 3)])  54.6 us
    ppermute x9, starting transfers between devices, over_z(): inward = add(value, lax.ppermute(value, 'z', [(0, 1), (3, 2)]))  38.3 us
    ppermute x8, waiting for transfers between devices, reduce(): mine = over_z(add(near[0], lax.ppermute(near[1], 'y', SWAP)), z)  32.8 us
    ppermute x8, waiting for transfers between devices, reduce(): near = add(near, lax.ppermute(far, 'mp', SWAP))  30.9 us
    ppermute x8, waiting for transfers between devices, reduce(): side = lax.ppermute(mine, 'y', SWAP)  22.2 us
    ppermute x9, waiting for transfers between devices, over_z(): inward = add(value, lax.ppermute(value, 'z', [(0, 1), (3, 2)]))  20.1 us
    ppermute x8, waiting for transfers between devices, fetch(): near = lax.ppermute(own, 'mp', SWAP)  16.4 us
  transfers between devices with their start and end apart: 110, of which 45 were waited for; matrix products, arithmetic and copies ran while one was open for 2% of the time, Pallas kernels for 15%

profile of v1, /device:TPU:0, one launch (start us, length us, event | category | flops | bytes accessed | tf_op | source)
XLA Modules:
  0.0 565.8 jit_solution(2569647584421189382)
XLA Ops:
  19.6 12.6 %collective-permute-done.16.q0 = bf16[128,768]{1,0:T(8,128)(2,1)S(1)} collective-permute-done((bf16[128,768]{1,0:T(8,128)(2,1)S(1)}, bf16[128,768]{1,0:T(8,128)(2,1)S(1)}, u32[]{:S(2)}, u32[]{:S(2)}) %collective-permute-start.16) | collective-permute-done | bytes 196640 | tf_op jit(solution)/shard_map/ppermute | solution.py:515
  44.8 38.5 %spatial_forward.1 = (bf16[8,1536,256]{2,1,0:T(8,128)(2,1)}, bf16[8,512,256]{2,1,0:T(8,128)(2,1)}, f32[8,512,256]{2,1,0:T(8,128)}, bf16[8,512,256]{2,1,0:T(8,128)(2,1)}, f32[8,16,256]{2,1,0:T(8,128)}) custom-call(s32[2]{0:T(128)} %pad_add_fusion.place, bf16[2048,512]{1,0:T(8,128)(2,1)} %x_ref.3, f32[2,256,1]{2,1,0:T(8,128)} %copy.23.bias_ref, ...), custom_call_target="tpu_custom_call" | custom-call | flops 5368709120 | bytes 20072456 | tf_op jit(solution)/shard_map/spatial_forward/pallas_call | solution.py:472
  86.8 25.2 %mlp_forward.1 = (f32[8,512,256]{2,1,0:T(8,128)}, bf16[4,2048,512]{2,1,0:T(8,128)(2,1)}, bf16[4,2048,512]{2,1,0:T(8,128)(2,1)}) custom-call(s32[2]{0:T(128)} %pad_add_fusion.place, f32[8,512,256]{2,1,0:T(8,128)} %get-tuple-element.49.r_ref, bf16[8,512,256]{2,1,0:T(8,128)(2,1)} %get-tuple-element.50.a2_ref, bf16[2,512,1024]{2,1,0:T(8,128)(2,1)} %wu.5, ...), custom_call_target="tpu_custom_call" | custom-call | flops 8589934592 | bytes 33554440 | tf_op jit(solution)/shard_map/mlp_forward/pallas_call | solution.py:472
  113.9 15.8 %temporal_forward.1 = (bf16[8,1536,256]{2,1,0:T(8,128)(2,1)}, bf16[8,512,256]{2,1,0:T(8,128)(2,1)}, f32[8,512,256]{2,1,0:T(8,128)}, bf16[8,512,256]{2,1,0:T(8,128)(2,1)}) custom-call(s32[2]{0:T(128)} %pad_add_fusion.place, s32[2,4]{1,0:T(2,128)} %constant_dynamic-slice_fusion.1.clip_ref, f32[8,512,256]{2,1,0:T(8,128)} %get-tuple-element.51.x_ref, ...), custom_call_target="tpu_custom_call" | custom-call | flops 5153960960 | bytes 22036520 | tf_op jit(solution)/shard_map/temporal_forward/pallas_call | solution.py:472
  130.7 45.8 %mlp_both.1 = (bf16[2048,512]{1,0:T(8,128)(2,1)}, f32[8,512,256]{2,1,0:T(8,128)}, bf16[2,2,128,1024]{3,2,1,0:T(8,128)(2,1)}, bf16[2,2,128,1024]{3,2,1,0:T(8,128)...) custom-call(s32[2]{0:T(128)} %pad_add_fusion.place, ...), custom_call_target="tpu_custom_call" | custom-call | flops 25769803776 | bytes 25198600 | tf_op jit(solution)/shard_map/mlp_both/pallas_call | solution.py:472
  176.6 25.6 %temporal_back.1 = (f32[8,512,256]{2,1,0:T(8,128)}, bf16[2,2,128,768]{3,2,1,0:T(8,128)(2,1)}, bf16[2,2,128,768]{3,2,1,0:T(8,128)(2,1)}, bf16[2,2,64,512]{3,2,1,0...) custom-call(s32[2]{0:T(128)} %pad_add_fusion.place, s32[2,4]{1,0:T(2,128)} %constant_dynamic-slice_fusion.1.clip_ref, ...), custom_call_target="tpu_custom_call" | custom-call | flops 10307921920 | bytes 26247208 | tf_op jit(solution)/shard_map/temporal_back/pallas_call | solution.py:472
  202.2 33.5 %mlp_back.1 = (f32[8,512,256]{2,1,0:T(8,128)}, bf16[2,2,128,1024]{3,2,1,0:T(8,128)(2,1)}, bf16[2,2,128,1024]{3,2,1,0:T(8,128)(2,1)}, bf16[2,2,256,512]{3,2,1,0:T...) custom-call(s32[2]{0:T(128)} %pad_add_fusion.place, f32[8,512,256]{2,1,0:T(8,128)} %get-tuple-element.49.r_ref, ...), custom_call_target="tpu_custom_call" | custom-call | flops 17179869184 | bytes 41975816 | tf_op jit(solution)/shard_map/mlp_back/pallas_call | solution.py:472
  235.7 49.8 %spatial_back.1 = (f32[2048,512]{1,0:T(8,128)}, bf16[2,2,128,768]{3,2,1,0:T(8,128)(2,1)}, bf16[2,2,128,768]{3,2,1,0:T(8,128)(2,1)}, bf16[2,2,64,512]{3,2,1,0:T(8...) custom-call(s32[2]{0:T(128)} %pad_add_fusion.place, bf16[2048,512]{1,0:T(8,128)(2,1)} %x_ref.3, ...), custom_call_target="tpu_custom_call" | custom-call | flops 11274289152 | bytes 24283144 | tf_op jit(solution)/shard_map/spatial_back/pallas_call | solution.py:472
  316.6 4.3 collective-permute-done.58
  320.9 4.2 collective-permute-done.67
  325.2 8.6 %collective-permute-start.59 = (bf16[64,512]{1,0:T(8,128)(2,1)S(1)}, bf16[64,512]{1,0:T(8,128)(2,1)S(1)}, u32[]{:S(2)}, u32[]{:S(2)}) collective-permute-start(bf16[64,512]{1,0:T(8,128)(2,1)S(1)} %fusion.31), channel_id=1, source_target_pairs={{0,8},{24,16},{1,9},{25,17},{2,10},{26,18},{3,11},{27,19},{4,12},{... | collective-permute-start | bytes 196616 | tf_op jit(solution)/shard_map/ppermute | solution.py:530
  336.2 4.4 collective-permute-start.68
  345.3 15.3 %collective-permute-done.61 = bf16[64,512]{1,0:T(8,128)(2,1)S(1)} collective-permute-done((bf16[64,512]{1,0:T(8,128)(2,1)S(1)}, bf16[64,512]{1,0:T(8,128)(2,1)S(1)}, u32[]{:S(2)}, u32[]{:S(2)}) %collective-permute-start.61) | collective-permute-done | bytes 65568 | tf_op jit(solution)/shard_map/ppermute | solution.py:532
  361.9 4.8 collective-permute-done.70
  374.2 7.4 %collective-permute-done.39 = bf16[2,128,768]{2,1,0:T(8,128)(2,1)S(1)} collective-permute-done((bf16[2,128,768]{2,1,0:T(8,128)(2,1)S(1)}, bf16[2,128,768]{2,1,0:T(8,128)(2,1)S(1)}, u32[]{:S(2)}, u32[]{:S(2)}) %collective-permute-start.39) | collective-permute-done | bytes 393248 | tf_op jit(solution)/shard_map/ppermute | solution.py:540
  383.7 6.4 %collective-permute-done.48 = bf16[2,128,768]{2,1,0:T(8,128)(2,1)S(1)} collective-permute-done((bf16[2,128,768]{2,1,0:T(8,128)(2,1)S(1)}, bf16[2,128,768]{2,1,0:T(8,128)(2,1)S(1)}, u32[]{:S(2)}, u32[]{:S(2)}) %collective-permute-start.48) | collective-permute-done | bytes 393248 | tf_op jit(solution)/shard_map/ppermute | solution.py:540
  404.0 5.3 collective-permute-start.41
  414.6 9.1 %collective-permute-done.84 = bf16[2,128,1024]{2,1,0:T(8,128)(2,1)S(1)} collective-permute-done((bf16[2,128,1024]{2,1,0:T(8,128)(2,1)S(1)}, bf16[2,128,1024]{2,1,0:T(8,128)(2,1)S(1)}, u32[]{:S(2)}, u32[]{:S(2)}) %collective-permute-start.84) | collective-permute-done | bytes 524320 | tf_op jit(solution)/shard_map/ppermute | solution.py:540
  423.8 4.6 collective-permute-start.50
  437.4 7.0 %collective-permute-done.76 = bf16[128,1024]{1,0:T(8,128)(2,1)S(1)} collective-permute-done((bf16[128,1024]{1,0:T(8,128)(2,1)S(1)}, bf16[128,1024]{1,0:T(8,128)(2,1)S(1)}, u32[]{:S(2)}, u32[]{:S(2)}) %collective-permute-start.76) | collective-permute-done | bytes 262176 | tf_op jit(solution)/shard_map/ppermute | solution.py:541
  446.3 3.8 collective-permute-done.94
  451.9 3.8 collective-permute-done.85
  461.0 9.0 %collective-permute-done.43 = bf16[128,768]{1,0:T(8,128)(2,1)S(1)} collective-permute-done((bf16[128,768]{1,0:T(8,128)(2,1)S(1)}, bf16[128,768]{1,0:T(8,128)(2,1)S(1)}, u32[]{:S(2)}, u32[]{:S(2)}) %collective-permute-start.43) | collective-permute-done | bytes 196640 | tf_op jit(solution)/shard_map/ppermute | solution.py:532
  473.5 4.6 collective-permute-done.77
  478.1 4.4 collective-permute-start.86
  483.7 4.4 collective-permute-start.104
  497.5 18.7 %collective-permute-done.79 = bf16[128,1024]{1,0:T(8,128)(2,1)S(1)} collective-permute-done((bf16[128,1024]{1,0:T(8,128)(2,1)S(1)}, bf16[128,1024]{1,0:T(8,128)(2,1)S(1)}, u32[]{:S(2)}, u32[]{:S(2)}) %collective-permute-start.79) | collective-permute-done | bytes 262176 | tf_op jit(solution)/shard_map/ppermute | solution.py:532
  536.8 5.5 collective-permute-done.99.refs_10_
  542.8 5.1 collective-permute-done.90.refs_6_
  548.4 4.6 collective-permute-done.108.refs_14_
  553.8 3.9 finish.2
  559.3 6.1 %finish.3 = (f32[2,512,1024]{2,1,0:T(8,128)}, f32[2,1024,512]{2,1,0:T(8,128)}) custom-call(s32[2]{0:T(128)} %pad_add_fusion.place, bf16[128,1024]{1,0:T(8,128)(2,1)} %copy-done.6, bf16[128,1024]{1,0:T(8,128)(2,1)} %copy-done.15, bf16[128,1024]{1,0:T(8,128)(2,1)} %copy-done.14, bf16[128,1024]{1,0:T(8,128)(2,1)} %copy-done.22, bf16[128,1024]{1,0:T(8,128)(2,1)} %copy-done.8, ...), custom_call_target="tpu_custom_call" | custom-call | bytes 12582920 | tf_op jit(solution)/shard_map/finish/pallas_call | solution.py:472
  (432 shorter events, 160.8 us)
Async XLA Ops:
  13.2 19.3 %collective-permute-start.8 = (bf16[128,1024]{1,0:T(8,128)(2,1)S(1)}, bf16[128,1024]{1,0:T(8,128)(2,1)S(1)}, u32[]{:S(2)}, u32[]{:S(2)}) collective-permute-start(bf16[128,1024]{1,0:T(8,128)(2,1)S(1)} %get-tuple-element.93), channel_id=1, source_target_pairs={{0,1},{1,0},{2,3},{3,2},{4,5},{5,4},{6,7},{7,6},{8,9},{9,8},{10,11... | collective-permute-start | bytes 786440 | tf_op jit(solution)/shard_map/ppermute | solution.py:515
  13.4 21.4 %collective-permute-start.12 = (bf16[256,512]{1,0:T(8,128)(2,1)S(1)}, bf16[256,512]{1,0:T(8,128)(2,1)S(1)}, u32[]{:S(2)}, u32[]{:S(2)}) collective-permute-start(bf16[256,512]{1,0:T(8,128)(2,1)S(1)} %get-tuple-element.91), channel_id=1, source_target_pairs={{0,1},{1,0},{2,3},{3,2},{4,5},{5,4},{6,7},{7,6},{8,9},{9,8},{10,11... | collective-permute-start | bytes 786440 | tf_op jit(solution)/shard_map/ppermute | solution.py:515
  16.4 21.4 %collective-permute-start.24 = (bf16[128,1024]{1,0:T(8,128)(2,1)S(1)}, bf16[128,1024]{1,0:T(8,128)(2,1)S(1)}, u32[]{:S(2)}, u32[]{:S(2)}) collective-permute-start(bf16[128,1024]{1,0:T(8,128)(2,1)S(1)} %get-tuple-element.92), channel_id=1, source_target_pairs={{0,1},{1,0},{2,3},{3,2},{4,5},{5,4},{6,7},{7,6},{8,9},{9,8},{10,11... | collective-permute-start | bytes 786440 | tf_op jit(solution)/shard_map/ppermute | solution.py:515
  17.3 20.5 %collective-permute-start.2 = (bf16[128,768]{1,0:T(8,128)(2,1)S(1)}, bf16[128,768]{1,0:T(8,128)(2,1)S(1)}, u32[]{:S(2)}, u32[]{:S(2)}) collective-permute-start(bf16[128,768]{1,0:T(8,128)(2,1)S(1)} %collective-permute-done.q0), channel_id=1, source_target_pairs={{0,4},{4,0},{1,5},{5,1},{2,6},{6,2},{3,7},{7,3},{8,12},{12,8},{9,1... | collective-permute-start | bytes 589832 | tf_op jit(solution)/shard_map/ppermute | solution.py:516
  42.0 41.3 %collective-permute-start.18 = (bf16[128,768]{1,0:T(8,128)(2,1)S(1)}, bf16[128,768]{1,0:T(8,128)(2,1)S(1)}, u32[]{:S(2)}, u32[]{:S(2)}) collective-permute-start(bf16[128,768]{1,0:T(8,128)(2,1)S(1)} %collective-permute-done.16.q0), channel_id=1, source_target_pairs={{0,4},{4,0},{1,5},{5,1},{2,6},{6,2},{3,7},{7,3},{8,12},{12,8},{9,1... | collective-permute-start | bytes 589832 | tf_op jit(solution)/shard_map/ppermute | solution.py:516
  43.5 40.4 %collective-permute-start.9 = (bf16[128,1024]{1,0:T(8,128)(2,1)S(1)}, bf16[128,1024]{1,0:T(8,128)(2,1)S(1)}, u32[]{:S(2)}, u32[]{:S(2)}) collective-permute-start(bf16[128,1024]{1,0:T(8,128)(2,1)S(1)} %collective-permute-done.8.u0), channel_id=1, source_target_pairs={{0,2},{2,0},{1,3},{3,1},{4,6},{6,4},{5,7},{7,5},{8,10},{10,8},{9,1... | collective-permute-start | bytes 786440 | tf_op jit(solution)/shard_map/ppermute | solution.py:519
  43.5 40.5 %collective-permute-start.13 = (bf16[256,512]{1,0:T(8,128)(2,1)S(1)}, bf16[256,512]{1,0:T(8,128)(2,1)S(1)}, u32[]{:S(2)}, u32[]{:S(2)}) collective-permute-start(bf16[256,512]{1,0:T(8,128)(2,1)S(1)} %collective-permute-done.12.d0), channel_id=1, source_target_pairs={{0,2},{2,0},{1,3},{3,1},{4,6},{6,4},{5,7},{7,5},{8,10},{10,8},{9,1... | collective-permute-start | bytes 786440 | tf_op jit(solution)/shard_map/ppermute | solution.py:519
  44.0 40.6 %collective-permute-start.11 = (bf16[128,1024]{1,0:T(8,128)(2,1)S(1)}, bf16[128,1024]{1,0:T(8,128)(2,1)S(1)}, u32[]{:S(2)}, u32[]{:S(2)}) collective-permute-start(bf16[128,1024]{1,0:T(8,128)(2,1)S(1)} %collective-permute-done.10.u2), channel_id=1, source_target_pairs={{0,2},{2,0},{1,3},{3,1},{4,6},{6,4},{5,7},{7,5},{8,10},{10,8},{9,1... | collective-permute-start | bytes 786440 | tf_op jit(solution)/shard_map/ppermute | solution.py:521
  44.1 42.0 %collective-permute-start.15 = (bf16[256,512]{1,0:T(8,128)(2,1)S(1)}, bf16[256,512]{1,0:T(8,128)(2,1)S(1)}, u32[]{:S(2)}, u32[]{:S(2)}) collective-permute-start(bf16[256,512]{1,0:T(8,128)(2,1)S(1)} %collective-permute-done.14.d2), channel_id=1, source_target_pairs={{0,2},{2,0},{1,3},{3,1},{4,6},{6,4},{5,7},{7,5},{8,10},{10,8},{9,1... | collective-permute-start | bytes 786440 | tf_op jit(solution)/shard_map/ppermute | solution.py:521
  83.4 28.6 %collective-permute-start.23 = (bf16[64,512]{1,0:T(8,128)(2,1)S(1)}, bf16[64,512]{1,0:T(8,128)(2,1)S(1)}, u32[]{:S(2)}, u32[]{:S(2)}) collective-permute-start(bf16[64,512]{1,0:T(8,128)(2,1)S(1)} %collective-permute-done.22.o2), channel_id=1, source_target_pairs={{0,2},{2,0},{1,3},{3,1},{4,6},{6,4},{5,7},{7,5},{8,10},{10,8},{9,1... | collective-permute-start | bytes 196616 | tf_op jit(solution)/shard_map/ppermute | solution.py:521
  83.9 28.2 %collective-permute-start.17 = (bf16[128,768]{1,0:T(8,128)(2,1)S(1)}, bf16[128,768]{1,0:T(8,128)(2,1)S(1)}, u32[]{:S(2)}, u32[]{:S(2)}) collective-permute-start(bf16[128,768]{1,0:T(8,128)(2,1)S(1)} %collective-permute-done.16.q0), channel_id=1, source_target_pairs={{0,2},{2,0},{1,3},{3,1},{4,6},{6,4},{5,7},{7,5},{8,10},{10,8},{9,1... | collective-permute-start | bytes 589832 | tf_op jit(solution)/shard_map/ppermute | solution.py:519
  84.0 28.7 %collective-permute-start.26 = (bf16[128,1024]{1,0:T(8,128)(2,1)S(1)}, bf16[128,1024]{1,0:T(8,128)(2,1)S(1)}, u32[]{:S(2)}, u32[]{:S(2)}) collective-permute-start(bf16[128,1024]{1,0:T(8,128)(2,1)S(1)} %collective-permute-done.24.u0), channel_id=1, source_target_pairs={{0,4},{4,0},{1,5},{5,1},{2,6},{6,2},{3,7},{7,3},{8,12},{12,8},{9,1... | collective-permute-start | bytes 786440 | tf_op jit(solution)/shard_map/ppermute | solution.py:516
  84.6 28.2 %collective-permute-start.30 = (bf16[256,512]{1,0:T(8,128)(2,1)S(1)}, bf16[256,512]{1,0:T(8,128)(2,1)S(1)}, u32[]{:S(2)}, u32[]{:S(2)}) collective-permute-start(bf16[256,512]{1,0:T(8,128)(2,1)S(1)} %collective-permute-done.28.d0), channel_id=1, source_target_pairs={{0,4},{4,0},{1,5},{5,1},{2,6},{6,2},{3,7},{7,3},{8,12},{12,8},{9,1... | collective-permute-start | bytes 786440 | tf_op jit(solution)/shard_map/ppermute | solution.py:516
  86.1 27.1 %collective-permute-start.19 = (bf16[128,768]{1,0:T(8,128)(2,1)S(1)}, bf16[128,768]{1,0:T(8,128)(2,1)S(1)}, u32[]{:S(2)}, u32[]{:S(2)}) collective-permute-start(bf16[128,768]{1,0:T(8,128)(2,1)S(1)} %collective-permute-done.18.q2), channel_id=1, source_target_pairs={{0,2},{2,0},{1,3},{3,1},{4,6},{6,4},{5,7},{7,5},{8,10},{10,8},{9,1... | collective-permute-start | bytes 589832 | tf_op jit(solution)/shard_map/ppermute | solution.py:521
  112.0 17.7 %collective-permute-start.25 = (bf16[128,1024]{1,0:T(8,128)(2,1)S(1)}, bf16[128,1024]{1,0:T(8,128)(2,1)S(1)}, u32[]{:S(2)}, u32[]{:S(2)}) collective-permute-start(bf16[128,1024]{1,0:T(8,128)(2,1)S(1)} %collective-permute-done.24.u0), channel_id=1, source_target_pairs={{0,2},{2,0},{1,3},{3,1},{4,6},{6,4},{5,7},{7,5},{8,10},{10,8},{9,1... | collective-permute-start | bytes 786440 | tf_op jit(solution)/shard_map/ppermute | solution.py:519
  112.2 17.6 %collective-permute-start.29 = (bf16[256,512]{1,0:T(8,128)(2,1)S(1)}, bf16[256,512]{1,0:T(8,128)(2,1)S(1)}, u32[]{:S(2)}, u32[]{:S(2)}) collective-permute-start(bf16[256,512]{1,0:T(8,128)(2,1)S(1)} %collective-permute-done.28.d0), channel_id=1, source_target_pairs={{0,2},{2,0},{1,3},{3,1},{4,6},{6,4},{5,7},{7,5},{8,10},{10,8},{9,1... | collective-permute-start | bytes 786440 | tf_op jit(solution)/shard_map/ppermute | solution.py:519
  303.5 63.3 %collective-permute-start.38 = (bf16[2,2,128,768]{3,2,1,0:T(8,128)(2,1)}, bf16[2,2,128,768]{3,2,1,0:T(8,128)(2,1)S(1)}, u32[]{:S(2)}, u32[]{:S(2)}) collective-permute-start(bf16[2,2,128,768]{3,2,1,0:T(8,128)(2,1)} %get-tuple-element.71), channel_id=1, source_target_pairs={{0,2},{2,0},{1,3},{3,1},{4,6},{6,4},{5,7},{7,5},{8,10},{10,8},{9,1... | collective-permute-start | bytes 2359304 | tf_op jit(solution)/shard_map/ppermute | solution.py:537
  303.6 64.0 %collective-permute-start.47 = (bf16[2,2,128,768]{3,2,1,0:T(8,128)(2,1)}, bf16[2,2,128,768]{3,2,1,0:T(8,128)(2,1)S(1)}, u32[]{:S(2)}, u32[]{:S(2)}) collective-permute-start(bf16[2,2,128,768]{3,2,1,0:T(8,128)(2,1)} %get-tuple-element.73), channel_id=1, source_target_pairs={{0,2},{2,0},{1,3},{3,1},{4,6},{6,4},{5,7},{7,5},{8,10},{10,8},{9,1... | collective-permute-start | bytes 2359304 | tf_op jit(solution)/shard_map/ppermute | solution.py:537
  304.1 65.3 %collective-permute-start.74 = (bf16[2,2,128,1024]{3,2,1,0:T(8,128)(2,1)}, bf16[2,2,128,1024]{3,2,1,0:T(8,128)(2,1)S(1)}, u32[]{:S(2)}, u32[]{:S(2)}) collective-permute-start(bf16[2,2,128,1024]{3,2,1,0:T(8,128)(2,1)} %get-tuple-element.81), channel_id=1, source_target_pairs={{0,2},{2,0},{1,3},{3,1},{4,6},{6,4},{5,7},{7,5},{8,10},{10,8},{9,1... | collective-permute-start | bytes 3145736 | tf_op jit(solution)/shard_map/ppermute | solution.py:537
  304.2 65.5 %collective-permute-start.92 = (bf16[2,2,256,512]{3,2,1,0:T(8,128)(2,1)}, bf16[2,2,256,512]{3,2,1,0:T(8,128)(2,1)S(1)}, u32[]{:S(2)}, u32[]{:S(2)}) collective-permute-start(bf16[2,2,256,512]{3,2,1,0:T(8,128)(2,1)} %get-tuple-element.85), channel_id=1, source_target_pairs={{0,2},{2,0},{1,3},{3,1},{4,6},{6,4},{5,7},{7,5},{8,10},{10,8},{9,1... | collective-permute-start | bytes 3145736 | tf_op jit(solution)/shard_map/ppermute | solution.py:537
  367.5 129.5 %collective-permute-start.37 = (f32[4,2,512]{2,1,0:T(2,128)S(1)}, f32[4,2,512]{2,1,0:T(2,128)S(1)}, u32[]{:S(2)}, u32[]{:S(2)}) collective-permute-start(f32[4,2,512]{2,1,0:T(2,128)S(1)} %add.212), channel_id=1, source_target_pairs={{8,0},{16,24},{9,1},{17,25},{10,2},{18,26},{11,3},{19,27},{12,4},{... | collective-permute-start | bytes 49160 | tf_op jit(solution)/shard_map/ppermute | solution.py:532
  369.3 128.1 %collective-permute-start.63 = (bf16[64,512]{1,0:T(8,128)(2,1)S(1)}, bf16[64,512]{1,0:T(8,128)(2,1)S(1)}, u32[]{:S(2)}, u32[]{:S(2)}) collective-permute-start(bf16[64,512]{1,0:T(8,128)(2,1)S(1)} %broadcast_select_fusion.7.refs_8_), channel_id=1, source_target_pairs={{0,4},{4,0},{1,5},{5,1},{2,6},{6,2},{3,7},{7,3},{8,12},{12,8},{9,1... | collective-permute-start | bytes 196616 | tf_op jit(solution)/shard_map/ppermute | solution.py:542
  371.7 18.4 %collective-permute-start.48 = (bf16[2,128,768]{2,1,0:T(8,128)(2,1)S(1)}, bf16[2,128,768]{2,1,0:T(8,128)(2,1)S(1)}, u32[]{:S(2)}, u32[]{:S(2)}) collective-permute-start(bf16[2,128,768]{2,1,0:T(8,128)(2,1)S(1)} %fusion.21), channel_id=1, source_target_pairs={{0,1},{1,0},{2,3},{3,2},{4,5},{5,4},{6,7},{7,6},{8,9},{9,8},{10,11... | collective-permute-start | bytes 1179656 | tf_op jit(solution)/shard_map/ppermute | solution.py:540
  372.2 31.8 %collective-permute-start.75 = (bf16[2,128,1024]{2,1,0:T(8,128)(2,1)S(1)}, bf16[2,128,1024]{2,1,0:T(8,128)(2,1)S(1)}, u32[]{:S(2)}, u32[]{:S(2)}) collective-permute-start(bf16[2,128,1024]{2,1,0:T(8,128)(2,1)S(1)} %fusion.7), channel_id=1, source_target_pairs={{0,1},{1,0},{2,3},{3,2},{4,5},{5,4},{6,7},{7,6},{8,9},{9,8},{10,11... | collective-permute-start | bytes 1572872 | tf_op jit(solution)/shard_map/ppermute | solution.py:540
  381.6 30.9 %collective-permute-start.93 = (bf16[2,256,512]{2,1,0:T(8,128)(2,1)S(1)}, bf16[2,256,512]{2,1,0:T(8,128)(2,1)S(1)}, u32[]{:S(2)}, u32[]{:S(2)}) collective-permute-start(bf16[2,256,512]{2,1,0:T(8,128)(2,1)S(1)} %fusion.11), channel_id=1, source_target_pairs={{0,1},{1,0},{2,3},{3,2},{4,5},{5,4},{6,7},{7,6},{8,9},{9,8},{10,11... | collective-permute-start | bytes 1572872 | tf_op jit(solution)/shard_map/ppermute | solution.py:540
  401.7 22.1 %collective-permute-start.84 = (bf16[2,128,1024]{2,1,0:T(8,128)(2,1)S(1)}, bf16[2,128,1024]{2,1,0:T(8,128)(2,1)S(1)}, u32[]{:S(2)}, u32[]{:S(2)}) collective-permute-start(bf16[2,128,1024]{2,1,0:T(8,128)(2,1)S(1)} %fusion.9), channel_id=1, source_target_pairs={{0,1},{1,0},{2,3},{3,2},{4,5},{5,4},{6,7},{7,6},{8,9},{9,8},{10,11... | collective-permute-start | bytes 1572872 | tf_op jit(solution)/shard_map/ppermute | solution.py:540
  412.5 105.0 %collective-permute-start.62 = (bf16[64,512]{1,0:T(8,128)(2,1)S(1)}, bf16[64,512]{1,0:T(8,128)(2,1)S(1)}, u32[]{:S(2)}, u32[]{:S(2)}) collective-permute-start(bf16[64,512]{1,0:T(8,128)(2,1)S(1)} %broadcast_select_fusion.7.refs_8_), channel_id=1, source_target_pairs={{0,2},{2,0},{1,3},{3,1},{4,6},{6,4},{5,7},{7,5},{8,10},{10,8},{9,1... | collective-permute-start | bytes 196616 | tf_op jit(solution)/shard_map/ppermute | solution.py:543
  412.5 21.7 %collective-permute-start.102 = (bf16[2,256,512]{2,1,0:T(8,128)(2,1)S(1)}, bf16[2,256,512]{2,1,0:T(8,128)(2,1)S(1)}, u32[]{:S(2)}, u32[]{:S(2)}) collective-permute-start(bf16[2,256,512]{2,1,0:T(8,128)(2,1)S(1)} %fusion.13), channel_id=1, source_target_pairs={{0,1},{1,0},{2,3},{3,2},{4,5},{5,4},{6,7},{7,6},{8,9},{9,8},{10,11... | collective-permute-start | bytes 1572872 | tf_op jit(solution)/shard_map/ppermute | solution.py:540
  494.3 21.8 %collective-permute-start.79 = (bf16[128,1024]{1,0:T(8,128)(2,1)S(1)}, bf16[128,1024]{1,0:T(8,128)(2,1)S(1)}, u32[]{:S(2)}, u32[]{:S(2)}) collective-permute-start(bf16[128,1024]{1,0:T(8,128)(2,1)S(1)} %add_convert_fusion.18), channel_id=1, source_target_pairs={{8,0},{16,24},{9,1},{17,25},{10,2},{18,26},{11,3},{19,27},{12,4},{... | collective-permute-start | bytes 786440 | tf_op jit(solution)/shard_map/ppermute | solution.py:532
  495.7 26.1 %collective-permute-start.97 = (bf16[256,512]{1,0:T(8,128)(2,1)S(1)}, bf16[256,512]{1,0:T(8,128)(2,1)S(1)}, u32[]{:S(2)}, u32[]{:S(2)}) collective-permute-start(bf16[256,512]{1,0:T(8,128)(2,1)S(1)} %add_convert_fusion.14), channel_id=1, source_target_pairs={{8,0},{16,24},{9,1},{17,25},{10,2},{18,26},{11,3},{19,27},{12,4},{... | collective-permute-start | bytes 786440 | tf_op jit(solution)/shard_map/ppermute | solution.py:532
  497.1 20.5 %collective-permute-start.72 = (bf16[64,512]{1,0:T(8,128)(2,1)S(1)}, bf16[64,512]{1,0:T(8,128)(2,1)S(1)}, u32[]{:S(2)}, u32[]{:S(2)}) collective-permute-start(bf16[64,512]{1,0:T(8,128)(2,1)S(1)} %broadcast_select_fusion.6.refs_12_), channel_id=1, source_target_pairs={{0,4},{4,0},{1,5},{5,1},{2,6},{6,2},{3,7},{7,3},{8,12},{12,8},{9,1... | collective-permute-start | bytes 196616 | tf_op jit(solution)/shard_map/ppermute | solution.py:542
  497.4 20.7 %collective-permute-start.71 = (bf16[64,512]{1,0:T(8,128)(2,1)S(1)}, bf16[64,512]{1,0:T(8,128)(2,1)S(1)}, u32[]{:S(2)}, u32[]{:S(2)}) collective-permute-start(bf16[64,512]{1,0:T(8,128)(2,1)S(1)} %broadcast_select_fusion.6.refs_12_), channel_id=1, source_target_pairs={{0,2},{2,0},{1,3},{3,1},{4,6},{6,4},{5,7},{7,5},{8,10},{10,8},{9,1... | collective-permute-start | bytes 196616 | tf_op jit(solution)/shard_map/ppermute | solution.py:543
  (155 other events, 2836.1 us)
